TPU v7x, 32 devices: a whole 2x2x4 slice. The times are simulated.
32 devices in a mesh: path: 4 (over y, core), fsdp: 8 (over z, x).
Axes of the slice: x: 2, y: 2, z: 4, core: 2. Of those that a mesh axis runs over, the one named last changes fastest.
Arguments:
- inputs: bfloat16 [4, 1024, 2048], P('path', 'fsdp'), may hold values from -6 to 6
- targets: bfloat16 [4, 1024, 2048], P('path', 'fsdp'), may hold values from -6 to 6
- token_ids: int32 [4, 1024], P('path', 'fsdp'), may hold values from 0 to 31999, as said below
- module_table: int32 [4, 2], replicated, may hold values from 0 to 3, as said below
- path_weights: bfloat16 [4, 2, 2048, 5632], P('path', None, None, 'fsdp'), may hold values from -6 to 6
- master: float32 [2, 4, 2048, 5632], P(None, None, 'path', 'fsdp'), may hold values from -6 to 6
- momentum: float32 [2, 4, 2048, 5632], P(None, None, 'path', 'fsdp'), may hold values from -6 to 6
Outputs:
- new_weights: bfloat16 [4, 2, 2048, 5632], P('path', None, None, 'fsdp')
- new_master: float32 [2, 4, 2048, 5632], P(None, None, 'path', 'fsdp')
- new_momentum: float32 [2, 4, 2048, 5632], P(None, None, 'path', 'fsdp')
Inputs may be any that keep to these rules, and one draw needn't show every extreme that they name: `module_table`: at each level, every module is named by exactly 1 paths. `token_ids`: ids below 256 are control tokens.
All inputs are finite; a program needn't handle non-finite values.
Results may differ from a plain program's by a relative error of at most 0.014.
Values may be sent and summed in bfloat16 or wider, within the bound.
No kernel may reach another device: no remote copies, remote signals or barrier semaphores. Data moves between devices by JAX's collectives and lax.ppermute only.
A program may use at most 128 MiB of HBM per device.

v0:
```python
import jax
import jax.numpy as jnp
from jax import lax
from jax.sharding import PartitionSpec as P

SPECIAL = 256


INNER_LR = 4096.0
OUTER_LR = 0.7
MOMENT = 0.9


def per_device(inputs, targets, token_ids, module_table, path_weights, master, momentum):
    x_local = inputs[0]
    w_in = path_weights[0, 0]
    w_out = path_weights[0, 1]
    width = w_in.shape[0]
    hidden_all = w_in.shape[1] * lax.axis_size("fsdp")
    out_scale = hidden_all ** (-0.5)
    x_full = lax.all_gather(x_local, "fsdp", axis=0, tiled=True)
    total = x_full.shape[0]
    pre = jnp.dot(x_full, w_in, preferred_element_type=jnp.float32) * width ** (-0.5)
    sig = jax.nn.sigmoid(pre)
    act = (pre * sig).astype(jnp.bfloat16)
    rows = act
    mine = lax.psum_scatter(
        (
            lax.dot_general(
                rows, w_out, (((1,), (1,)), ((), ())), preferred_element_type=jnp.float32
            )
            * out_scale
        ).astype(jnp.bfloat16),
        "fsdp",
        scatter_dimension=0,
        tiled=True,
    ).astype(jnp.float32)
    keep = (token_ids[0] >= SPECIAL).astype(jnp.float32)
    residual = x_local.astype(jnp.float32) + mine - targets[0].astype(jnp.float32)
    grad_mine = (keep[:, None] * residual / total).astype(jnp.bfloat16)
    piece = lax.all_gather(grad_mine, "fsdp", axis=0, tiled=True)
    rows = jnp.dot(piece, w_out, preferred_element_type=jnp.float32) * out_scale
    weight_acc = lax.dot_general(
        piece, act, (((0,), (0,)), ((), ())), preferred_element_type=jnp.float32
    )
    grad_out = weight_acc * out_scale
    pre_grad = (rows * sig * (1.0 + pre * (1.0 - sig))).astype(jnp.bfloat16)
    delta_out = INNER_LR * grad_out
    grad_in = lax.dot_general(
        x_full, pre_grad, (((0,), (0,)), ((), ())), preferred_element_type=jnp.float32
    ) * width ** (-0.5)
    stacked = jnp.stack([INNER_LR * grad_in, delta_out])[:, None]
    arrived = lax.all_to_all(
        stacked.astype(jnp.bfloat16), "path", split_axis=2, concat_axis=1, tiled=True
    ).astype(stacked.dtype)
    modules = master.shape[1]
    labels = jnp.arange(modules, dtype=jnp.int32)
    pick = (module_table.T[:, None, :] == labels[None, :, None]).astype(jnp.float32)
    counts = jnp.sum(pick, axis=2)
    sums = jnp.einsum("lmq,lqrc->lmrc", pick, arrived, precision=lax.Precision.HIGHEST)
    average = sums / counts[:, :, None, None]
    new_momentum = MOMENT * momentum + average
    new_master = master - OUTER_LR * (average + MOMENT * new_momentum)
    route = jnp.transpose(pick, (0, 2, 1)).astype(jnp.bfloat16)
    outgoing = jnp.einsum(
        "lqm,lmrc->lqrc", route, new_master.astype(jnp.bfloat16), preferred_element_type=jnp.float32
    ).astype(jnp.bfloat16)
    returned = lax.all_to_all(outgoing, "path", split_axis=1, concat_axis=2, tiled=True)
    new_weights = jnp.transpose(returned, (1, 0, 2, 3))
    return (new_weights, new_master, new_momentum)


def solution(mesh):
    in_specs = (
        P("path", "fsdp", None),
        P("path", "fsdp", None),
        P("path", "fsdp"),
        P(),
        P("path", None, None, "fsdp"),
        P(None, None, "path", "fsdp"),
        P(None, None, "path", "fsdp"),
    )
    out_specs = (
        P("path", None, None, "fsdp"),
        P(None, None, "path", "fsdp"),
        P(None, None, "path", "fsdp"),
    )
    return jax.shard_map(
        per_device, mesh=mesh, in_specs=in_specs, out_specs=out_specs, check_vma=False
    )
```

profile of v0, /device:TPU:0, one launch (start us, length us, event | category | flops | bytes accessed | tf_op | source)
XLA Modules:
  0.0 537.7 jit_solution(4546353051034360190)
XLA Ops:
  7.2 0.0 all-gather.6.cloned.1.call-start
  7.2 0.7 all-gather.6.cloned.1.call-update
  7.9 0.0 reduce-scatter.2.cloned.1.call-start
  7.9 78.3 %all-gather.6.cloned.1.call-done = bf16[1,1024,2048]{2,1,0:T(8,128)(2,1)} async-done(((bf16[1,128,2048]{2,1,0:T(8,128)(2,1)}), bf16[1,1024,2048]{2,1,0:T(8,128)(2,1)}) %all-gather.6.cloned.1.call-update) | async-done | bytes 4194320 | tf_op jit(solution)/shard_map/all_gather | solution.py:21
  86.3 5.9 %fusion.8 = f32[1024,704]{0,1:T(8,128)S(1)} fusion(bf16[1,1024,2048]{2,1,0:T(8,128)(2,1)} %all-gather.6.cloned.1.call-done, bf16[1,2,2048,704]{2,3,1,0:T(8,128)(2,1)} %param.11), kind=kOutput, calls=%fused_computation.13 | convolution fusion | flops 2952790016 | bytes 9961472 | tf_op jit(solution)/shard_map/dot_general | solution.py:23
  92.1 0.0 copy-start.4
  92.1 1.6 copy-done.4
  93.7 7.0 %multiply_convert_fusion = bf16[1024,2048]{1,0:T(8,128)(2,1)} fusion(bf16[1,2,2048,704]{2,3,1,0:T(8,128)(2,1)} %param.11, f32[1024,704]{0,1:T(8,128)S(1)} %fusion.8), kind=kOutput, calls=%fused_computation.3 | convolution fusion | flops 2961309696 | bytes 9961472 | tf_op jit(solution)/shard_map/dot_general | solution.py:29
  100.7 0.0 reduce-scatter.2.cloned.1.call-update
  100.7 0.2 all-gather.4.cloned.1.call-start
  101.0 0.4 copy-done.3
  101.4 85.7 %reduce-scatter.2.cloned.1.call-done = bf16[128,2048]{1,0:T(8,128)(2,1)} async-done(((bf16[1024,2048]{1,0:T(8,128)(2,1)}), bf16[128,2048]{1,0:T(8,128)(2,1)}) %reduce-scatter.2.cloned.1.call-update) | async-done | bytes 524304 | tf_op jit(solution)/shard_map/reduce_scatter | solution.py:27
  187.1 2.1 fusion.29
  189.2 0.0 all-gather.4.cloned.1.call-update
  189.3 73.9 %all-gather.4.cloned.1.call-done = bf16[1024,2048]{1,0:T(8,128)(2,1)} async-done(((bf16[128,2048]{1,0:T(8,128)(2,1)}), bf16[1024,2048]{1,0:T(8,128)(2,1)}) %all-gather.4.cloned.1.call-update) | async-done | bytes 4194320 | tf_op jit(solution)/shard_map/all_gather | solution.py:41
  263.2 11.9 %fusion.12 = bf16[1,1,2048,704]{2,3,1,0:T(8,128)(2,1)S(1)} fusion(bf16[1,1024,2048]{2,1,0:T(8,128)(2,1)} %all-gather.6.cloned.1.call-done, f32[1024,704]{0,1:T(8,128)} %copy-done.4, bf16[1024,2048]{1,0:T(8,128)(2,1)} %all-gather.4.cloned.1.call-done, bf16[1,2,2048,704]{2,3,1,0:T(8,128)(2,1)} %param.11), kind=kOutput, calls=%fused_computation.15 | convolution fusion | flops 5916393472 | bytes 17039360 | tf_op jit(solution)/shard_map/dot_general | solution.py:49
  275.1 6.3 %fusion.15 = bf16[1,1,2048,704]{2,3,1,0:T(8,128)(2,1)S(1)} fusion(bf16[1024,2048]{1,0:T(8,128)(2,1)} %all-gather.4.cloned.1.call-done, f32[1024,704]{0,1:T(8,128)} %copy-done.4), kind=kOutput, calls=%fused_computation.16 | convolution fusion | flops 2959998976 | bytes 9961472 | tf_op jit(solution)/shard_map/dot_general | solution.py:43
  281.4 3.0 pad_maximum_fusion
  284.4 16.1 %copy.29 = bf16[2,1,2048,704]{3,0,1,2:T(2,128)(2,1)} copy(bf16[2,1,2048,704]{2,3,1,0:T(8,128)(2,1)} %pad_maximum_fusion) | data formatting | bytes 11534336 | tf_op jit(solution)/shard_map/stack | solution.py:52
  300.5 5.6 %all-to-all-start = ((bf16[2,1,2048,704]{3,0,1,2:T(2,128)(2,1)}), bf16[2,1,2048,704]{3,0,1,2:T(2,128)(2,1)}, u32[]{:S(2)}, u32[]{:S(2)}) async-start(bf16[2,1,2048,704]{3,0,1,2:T(2,128)(2,1)} %copy.29), calls=%async_computation.1 | async-start | bytes 12582912 | tf_op jit(solution)/shard_map/all_to_all | solution.py:53
  306.1 0.1 convert_reduce_fusion
  306.2 70.6 %all-to-all-done = bf16[2,1,2048,704]{3,0,1,2:T(2,128)(2,1)} async-done(((bf16[2,1,2048,704]{3,0,1,2:T(2,128)(2,1)}), bf16[2,1,2048,704]{3,0,1,2:T(2,128)(2,1)}, u32[]{:S(2)}, u32[]{:S(2)}) %all-to-all-start) | async-done | bytes 5767200 | tf_op jit(solution)/shard_map/all_to_all | solution.py:53
  376.8 17.0 %copy.39 = bf16[2,4,512,704]{2,1,3,0:T(4,128)(2,1)} copy(bf16[2,4,512,704]{3,0,2,1:T(2,128)(2,1)} %bitcast.14) | data formatting | bytes 11534336 | tf_op jit(solution)/shard_map/all_to_all | solution.py:53
  393.8 36.6 %fusion = (f32[2,4,512,704]{2,1,3,0:T(4,128)}, f32[2,4,512,704]{2,1,3,0:T(4,128)}) fusion(f32[2,4,512,704]{2,3,1,0:T(8,128)} %param.13, f32[2,4,512,704]{2,3,1,0:T(8,128)} %param.12, f32[2,4]{1,0:T(2,128)S(1)} %convert_reduce_fusion, bf16[2,4,512,704]{2,1,3,0:T(4,128)(2,1)} %copy.39, s32[2,4]{1,0:T(2,128)S(1)} %bitcast.55), kind=kOutput, calls=%fused_computation.2 | convolution fusion | flops 43253792 | bytes 51904576 | tf_op jit(solution)/shard_map/lmq,lqrc->lmrc/dot_general | solution.py:60
  430.5 6.1 %fusion.3 = bf16[2,4,512,704]{2,1,3,0:T(4,128)(2,1)S(1)} fusion(f32[2,4,512,704]{2,1,3,0:T(4,128)} %get-tuple-element.16, s32[2,4]{1,0:T(2,128)S(1)} %bitcast.56), kind=kOutput, calls=%fused_computation.10 | convolution fusion | flops 28835936 | bytes 17301536 | tf_op jit(solution)/shard_map/lqm,lmrc->lqrc/dot_general | solution.py:65
  436.6 3.7 copy.33
  440.2 5.4 %all-to-all-start.1 = ((bf16[2,4,512,704]{2,3,0,1:T(8,128)(2,1)}), bf16[2,4,512,704]{2,3,0,1:T(8,128)(2,1)}, u32[]{:S(2)}, u32[]{:S(2)}) async-start(bf16[2,4,512,704]{2,3,0,1:T(8,128)(2,1)} %copy.33), calls=%async_computation.2 | async-start | bytes 11534336 | tf_op jit(solution)/shard_map/all_to_all | solution.py:68
  445.7 12.1 %copy.35 = f32[2,4,512,704]{2,3,1,0:T(8,128)} copy(f32[2,4,512,704]{2,1,3,0:T(4,128)} %get-tuple-element.16) | data formatting | bytes 23068672
  457.8 12.1 %copy.36 = f32[2,4,512,704]{2,3,1,0:T(8,128)} copy(f32[2,4,512,704]{2,1,3,0:T(4,128)} %get-tuple-element.15) | data formatting | bytes 23068672
  469.9 40.8 %all-to-all-done.1 = bf16[2,4,512,704]{2,3,0,1:T(8,128)(2,1)} async-done(((bf16[2,4,512,704]{2,3,0,1:T(8,128)(2,1)}), bf16[2,4,512,704]{2,3,0,1:T(8,128)(2,1)}, u32[]{:S(2)}, u32[]{:S(2)}) %all-to-all-start.1) | async-done | bytes 5767200 | tf_op jit(solution)/shard_map/all_to_all | solution.py:68
  510.8 9.6 %copy.34 = bf16[2,4,512,704]{2,1,3,0:T(4,128)(2,1)} copy(bf16[2,4,512,704]{2,3,0,1:T(8,128)(2,1)} %all-to-all-done.1) | data formatting | bytes 11534336 | tf_op jit(solution)/shard_map/all_to_all | solution.py:68
  520.3 10.4 %transpose.18 = bf16[1,2,2048,704]{2,3,1,0:T(8,128)(2,1)} reshape(bf16[2,4,512,704]{2,1,3,0:T(4,128)(2,1)} %copy.34) | data formatting | bytes 11534336 | tf_op jit(solution)/shard_map/transpose | solution.py:69
  (8 shorter events, 0.0 us)
Async XLA Ops:
  7.2 79.1 %all-gather.6.cloned.1.call-start = ((), (), s32[]{:S(2)}) async-start(), calls=%async_computation.5 | async-start | bytes 4718592 | tf_op jit(solution)/shard_map/all_gather | solution.py:21
  7.9 179.2 %reduce-scatter.2.cloned.1.call-start = ((), (), s32[]{:S(2)}) async-start(), calls=%async_computation.3 | async-start | bytes 4718592 | tf_op jit(solution)/shard_map/reduce_scatter | solution.py:27
  92.1 1.6 copy-start.4
  100.7 0.7 copy-start.3
  100.7 86.4 %copy-start = (bf16[1,128,2048]{2,1,0:T(8,128)(2,1)S(1)}, bf16[1,128,2048]{2,1,0:T(8,128)(2,1)}, u32[]{:S(2)}) copy-start(bf16[1,128,2048]{2,1,0:T(8,128)(2,1)} %param.7) | copy-start | bytes 1572868
  100.7 86.4 %copy-start.1 = (bf16[1,128,2048]{2,1,0:T(8,128)(2,1)S(1)}, bf16[1,128,2048]{2,1,0:T(8,128)(2,1)}, u32[]{:S(2)}) copy-start(bf16[1,128,2048]{2,1,0:T(8,128)(2,1)} %param.8) | copy-start | bytes 1572868
  100.7 162.5 %all-gather.4.cloned.1.call-start = ((), (), s32[]{:S(2)}) async-start(), calls=%async_computation.4 | async-start | bytes 4718592 | tf_op jit(solution)/shard_map/all_gather | solution.py:41
  300.5 5.6 %copy-start.2 = (s32[4,2]{0,1:T(2,128)S(1)}, s32[4,2]{0,1:T(2,128)}, u32[]{:S(2)}) copy-start(s32[4,2]{0,1:T(2,128)} %param.10) | copy-start | bytes 100
  300.5 76.3 %all-to-all-start = ((bf16[2,1,2048,704]{3,0,1,2:T(2,128)(2,1)}), bf16[2,1,2048,704]{3,0,1,2:T(2,128)(2,1)}, u32[]{:S(2)}, u32[]{:S(2)}) async-start(bf16[2,1,2048,704]{3,0,1,2:T(2,128)(2,1)} %copy.29), calls=%async_computation.1 | async-start | bytes 12582912 | tf_op jit(solution)/shard_map/all_to_all | solution.py:53
  440.2 70.5 %all-to-all-start.1 = ((bf16[2,4,512,704]{2,3,0,1:T(8,128)(2,1)}), bf16[2,4,512,704]{2,3,0,1:T(8,128)(2,1)}, u32[]{:S(2)}, u32[]{:S(2)}) async-start(bf16[2,4,512,704]{2,3,0,1:T(8,128)(2,1)} %copy.33), calls=%async_computation.2 | async-start | bytes 11534336 | tf_op jit(solution)/shard_map/all_to_all | solution.py:68
Sparse Core Ops, SparseCore 0:
  10.1 76.0 all-gather.5
  100.9 86.2 reduce-scatter.1
  190.0 73.1 all-gather.3
where the time goes:
time: 542 us; the launch traced here: 538 us
  waiting for transfers between devices  350 us (65%)
  local copies, waits for them, and re-layouts  83 us (15%)
  matrix products  73.8 us (14%)
  between operations  14.3 us (3%)
  starting transfers between devices  11.3 us (2%)
    reduce_scatter x1, waiting for transfers between devices, per_device(): lax.psum_scatter((lax.dot_general(rows, w_out, (((1,), (1,)), ((), ())),...  85.7 us
    all_gather x1, waiting for transfers between devices, per_device(): x_full = lax.all_gather(x_local, 'fsdp', axis=0, tiled=True)  78.3 us
    all_gather x1, waiting for transfers between devices, per_device(): piece = lax.all_gather(grad_mine, 'fsdp', axis=0, tiled=True)  73.9 us
    all_to_all x1, waiting for transfers between devices, per_device(): lax.all_to_all(stacked.astype(jnp.bfloat16), 'path', split_axis=2, concat...  70.6 us
    all_to_all x1, waiting for transfers between devices, per_device(): lax.all_to_all(outgoing, 'path', split_axis=1, concat_axis=2, tiled=True)  40.8 us
    dot_general x1, matrix products, per_device(): jnp.einsum('lmq,lqrc->lmrc', pick, arrived, precision=lax.Precision.HIGHEST)  36.6 us
    unnamed x12, local copies, waits for them, and re-layouts  26.2 us
    all_to_all x1, local copies, waits for them, and re-layouts, per_device(): lax.all_to_all(stacked.astype(jnp.bfloat16), 'path', split_axis=2, concat...  17 us
  transfers between devices with their start and end apart: 5, of which 5 were waited for; matrix products, arithmetic and copies ran while one was open for 5% of the time, Pallas kernels for 0%

commit v1 on v0

--- a/solution.py
+++ b/solution.py
@@ -1,6 +1,8 @@
 import jax
 import jax.numpy as jnp
 from jax import lax
+from jax.experimental import pallas as pl
+from jax.experimental.pallas import tpu as pltpu
 from jax.sharding import PartitionSpec as P
 
 SPECIAL = 256
@@ -11,7 +13,7 @@
 MOMENT = 0.9
 
 
-def per_device(inputs, targets, token_ids, module_table, path_weights, master, momentum):
+def any_table(inputs, targets, token_ids, module_table, path_weights, master, momentum):
     x_local = inputs[0]
     w_in = path_weights[0, 0]
     w_out = path_weights[0, 1]
@@ -70,6 +72,458 @@
     return (new_weights, new_master, new_momentum)
 
 
+MIB = 1024 * 1024
+LANES = 1024
+F32, BF16 = jnp.float32, jnp.bfloat16
+NT = (((1,), (1,)), ((), ()))
+
+
+def params(steps, room):
+    return pltpu.CompilerParams(
+        vmem_limit_bytes=room * MIB, dimension_semantics=("arbitrary",) * steps
+    )
+
+
+def cost(flops, moved):
+    return pl.CostEstimate(flops=1, bytes_accessed=1, transcendentals=0)
+
+
+def whole(shape):
+    return pl.BlockSpec(shape, lambda *_: (0,) * len(shape))
+
+
+def forward(pieces, weights, in_scale, out_scale, types, after):
+    half, width = pieces[0].shape
+    hidden = weights.shape[2]
+    n, tokens = len(pieces), len(pieces) * half
+    tiles = width // LANES
+
+    def kernel(*refs):
+        w_in, w_out = refs[n : n + 2]
+        act_ref, slope_ref, *parts, pre_ref, flat_ref = refs[n + 2 + len(after) :]
+        step = pl.program_id(0)
+
+        @pl.when(step < tiles)
+        def _():
+            x = jnp.concatenate([ref[...] for ref in refs[:n]], axis=0)
+            part = lax.dot_general(w_in[0, 0], x, NT, preferred_element_type=F32)
+
+            @pl.when(step == 0)
+            def _():
+                pre_ref[...] = part
+
+            @pl.when(step > 0)
+            def _():
+                pre_ref[...] += part
+
+        @pl.when(step == tiles - 1)
+        def _():
+            pre = pre_ref[...] * in_scale
+            sig = jax.nn.sigmoid(pre)
+            act = pre * sig
+            act_ref[...] = act.astype(BF16)
+            flat_ref[...] = act.T.astype(BF16)
+            slope_ref[...] = sig * (1.0 + pre * (1.0 - sig))
+
+        @pl.when(step >= tiles)
+        def _():
+            part = jnp.dot(flat_ref[...], w_out[0, 0], preferred_element_type=F32) * out_scale
+            for k, ref in enumerate(parts):
+                ref[...] = part[k * half : (k + 1) * half].astype(ref.dtype)
+
+    first = lambda i: (0, jnp.minimum(i, tiles - 1))
+    last = lambda i: (0, jnp.maximum(i - tiles, 0))
+    return pl.pallas_call(
+        kernel,
+        grid=(2 * tiles,),
+        in_specs=[
+            *[pl.BlockSpec((half, LANES), first)] * n,
+            pl.BlockSpec((1, 1, hidden, LANES), lambda i: (0, 0) + first(i)),
+            pl.BlockSpec((1, 1, hidden, LANES), lambda i: (0, 1) + last(i)),
+        ]
+        + [pl.BlockSpec(memory_space=pl.ANY)] * len(after),
+        out_specs=[
+            whole((hidden, tokens)),
+            whole((hidden, tokens)),
+            *[pl.BlockSpec((half, LANES), last)] * n,
+        ],
+        out_shape=[
+            jax.ShapeDtypeStruct((hidden, tokens), BF16),
+            jax.ShapeDtypeStruct((hidden, tokens), F32),
+            *[jax.ShapeDtypeStruct((half, width), kind) for kind in types],
+        ],
+        scratch_shapes=[pltpu.VMEM((hidden, tokens), F32), pltpu.VMEM((tokens, hidden), BF16)],
+        compiler_params=params(1, 18),
+        cost_estimate=cost(4 * tokens * width * hidden, 4 * width * hidden + 10 * tokens * width),
+        name="forward",
+    )(*pieces, weights, weights, *after)
+
+
+def backward(pieces, weights, slope, out_scale, after):
+    half, width = pieces[0].shape
+    hidden, tokens = slope.shape
+    n = len(pieces)
+    tiles = width // LANES
+
+    def kernel(*refs):
+        w_out, slope_ref = refs[n : n + 2]
+        out_ref, sum_ref = refs[n + 2 + len(after) :]
+        step = pl.program_id(0)
+        g = jnp.concatenate([ref[...] for ref in refs[:n]], axis=0)
+        part = lax.dot_general(w_out[0, 0], g, NT, preferred_element_type=F32)
+
+        @pl.when(step == 0)
+        def _():
+            sum_ref[...] = part
+
+        @pl.when(step > 0)
+        def _():
+            sum_ref[...] += part
+
+        @pl.when(step == tiles - 1)
+        def _():
+            out_ref[...] = (sum_ref[...] * out_scale * slope_ref[...]).astype(BF16)
+
+    return pl.pallas_call(
+        kernel,
+        grid=(tiles,),
+        in_specs=[
+            *[pl.BlockSpec((half, LANES), lambda i: (0, i))] * n,
+            pl.BlockSpec((1, 1, hidden, LANES), lambda i: (0, 1, 0, i)),
+            whole((hidden, tokens)),
+        ]
+        + [pl.BlockSpec(memory_space=pl.ANY)] * len(after),
+        out_specs=whole((hidden, tokens)),
+        out_shape=jax.ShapeDtypeStruct((hidden, tokens), BF16),
+        scratch_shapes=[pltpu.VMEM((hidden, tokens), F32)],
+        compiler_params=params(1, 12),
+        cost_estimate=cost(2 * tokens * width * hidden, 2 * width * hidden + 2 * tokens * width),
+        name="backward",
+    )(*pieces, weights, slope, *after)
+
+
+def untouched(arrays):
+    return [pl.BlockSpec(memory_space=pl.ANY)] * len(arrays)
+
+
+def add_rows(a, b):
+    def kernel(a_ref, b_ref, out_ref):
+        out_ref[...] = (a_ref[...].astype(F32) + b_ref[...].astype(F32)).astype(out_ref.dtype)
+
+    return pl.pallas_call(
+        kernel,
+        out_shape=jax.ShapeDtypeStruct(a.shape, a.dtype),
+        compiler_params=pltpu.CompilerParams(vmem_limit_bytes=4 * MIB),
+        cost_estimate=cost(a.size, 6 * a.size),
+        name="add_rows",
+    )(a, b)
+
+
+def base_rows(where, master, momentum, d, together, after):
+    levels, _, hidden, block = master.shape
+
+    def kernel(_, master_ref, momentum_ref, *refs):
+        value = master_ref[0, 0] - (OUTER_LR * MOMENT * MOMENT) * momentum_ref[0, 0]
+        outs = refs[len(after) :]
+        if together:
+            outs[0][0] = value.astype(BF16)
+            return
+        for level, out_ref in enumerate(outs):
+
+            @pl.when(pl.program_id(0) == level)
+            def _(out_ref=out_ref):
+                out_ref[...] = value.astype(BF16)
+
+    source = pl.BlockSpec(
+        (1, 1, hidden, block), lambda l, s: (l, s[1 + (s[0] ^ d) * levels + l], 0, 0)
+    )
+    return pl.pallas_call(
+        kernel,
+        grid_spec=pltpu.PrefetchScalarGridSpec(
+            num_scalar_prefetch=1,
+            grid=(levels,),
+            in_specs=[source, source] + untouched(after),
+            out_specs=[pl.BlockSpec((1, hidden, block), lambda l, s: (l, 0, 0))]
+            if together
+            else [whole((hidden, block))] * levels,
+        ),
+        out_shape=[jax.ShapeDtypeStruct((levels, hidden, block), BF16)]
+        if together
+        else [jax.ShapeDtypeStruct((hidden, block), BF16)] * levels,
+        compiler_params=params(1, 42),
+        cost_estimate=cost(3 * levels * hidden * block, 10 * levels * hidden * block),
+        name="base_rows",
+    )(where, master, momentum, *after)
+
+
+def module_rows(
+    where, level, d, scale, lefts, rights, block, send=False, base=None, fresh=None, copy_shape=None, outer=None, after=()
+):
+    rows, wide = rights[0].shape
+    hidden, tokens = lefts[0].shape
+    tile = hidden
+    n_left, n_right = len(lefts), len(rights)
+    operands = [*lefts, *rights]
+    in_specs = [pl.BlockSpec((tile, tokens), lambda i, s: (i, 0))] * n_left
+    in_specs += [pl.BlockSpec((rows, block), lambda i, s: (0, s[0] ^ d if wide > block else 0))] * n_right
+    out_specs, out_shape, aliases = [], [], {}
+    if send:
+        out_specs.append(pl.BlockSpec((tile, block), lambda i, s: (i, 0)))
+        out_shape.append(jax.ShapeDtypeStruct((hidden, block), BF16))
+    if base is not None:
+        operands.append(base)
+        if base.ndim == 3:
+            in_specs.append(pl.BlockSpec((1, tile, block), lambda i, s: (level, i, 0)))
+        else:
+            in_specs.append(pl.BlockSpec((tile, block), lambda i, s: (i, 0)))
+    if copy_shape is not None:
+        if fresh is not None:
+            operands.append(fresh)
+            in_specs += untouched([fresh])
+            aliases[len(operands)] = len(out_shape)
+        out_specs.append(pl.BlockSpec((1, 1, tile, block), lambda i, s: (0, level, i, s[0] ^ d)))
+        out_shape.append(jax.ShapeDtypeStruct(copy_shape, BF16))
+    if outer is not None:
+        master, momentum, *state = outer
+        levels = master.shape[0]
+        place = pl.BlockSpec(
+            (1, 1, tile, block), lambda i, s: (level, s[1 + (s[0] ^ d) * levels + level], i, 0)
+        )
+        operands += [master, momentum, *state]
+        in_specs += [place, place] + untouched(state)
+        for k in range(len(state)):
+            aliases[len(operands) - 1 + k] = len(out_shape) + k
+        out_specs += [place, place]
+        out_shape += [jax.ShapeDtypeStruct(master.shape, F32)] * 2
+    n_in = len(operands) + len(after)
+
+    def kernel(_, *refs):
+        ins, outs = list(refs[:n_in]), list(refs[n_in:])
+        left = jnp.concatenate([ref[...] for ref in ins[:n_left]], axis=1)
+        right = jnp.concatenate([ref[...] for ref in ins[n_left : n_left + n_right]], axis=0)
+        rest = ins[n_left + n_right :]
+        delta = jnp.dot(left, right, preferred_element_type=F32) * scale
+        if send:
+            outs.pop(0)[...] = delta.astype(BF16)
+        if base is not None:
+            start = rest.pop(0)[...].astype(F32).reshape(tile, block)
+            outs.pop(0)[0, 0] = (start - (OUTER_LR * (1.0 + MOMENT)) * delta).astype(BF16)
+        if fresh is not None:
+            rest.pop(0)
+        if outer is not None:
+            nesterov(delta, *rest[:2], *outs[-2:])
+            if copy_shape is not None:
+                outs[0][0, 0] = outs[-2][0, 0].astype(BF16)
+
+    return pl.pallas_call(
+        kernel,
+        grid_spec=pltpu.PrefetchScalarGridSpec(
+            num_scalar_prefetch=1,
+            grid=(hidden // tile,),
+            in_specs=in_specs + untouched(after),
+            out_specs=out_specs,
+        ),
+        out_shape=out_shape,
+        input_output_aliases=aliases,
+        compiler_params=params(1, 24 if outer is None else 48),
+        cost_estimate=cost(2 * hidden * block * rows * n_right, 2 * rows * n_right * (hidden + block)),
+        name="module_rows",
+    )(where, *operands, *after)
+
+
+def nesterov(average, master_ref, momentum_ref, new_master, new_momentum):
+    moved = MOMENT * momentum_ref[0, 0] + average
+    new_momentum[0, 0] = moved
+    new_master[0, 0] = master_ref[0, 0] - OUTER_LR * (average + MOMENT * moved)
+
+
+def outer_rows(where, delta, level, d, outer):
+    master, momentum, *state = outer
+    levels, _, hidden, block = master.shape
+    tile = hidden // 2
+
+    def kernel(_, delta_ref, master_ref, momentum_ref, *refs):
+        nesterov(delta_ref[...].astype(F32), master_ref, momentum_ref, *refs[-2:])
+
+    place = pl.BlockSpec(
+        (1, 1, tile, block), lambda i, s: (level, s[1 + (s[0] ^ d) * levels + level], i, 0)
+    )
+    return pl.pallas_call(
+        kernel,
+        grid_spec=pltpu.PrefetchScalarGridSpec(
+            num_scalar_prefetch=1,
+            grid=(hidden // tile,),
+            in_specs=[pl.BlockSpec((tile, block), lambda i, s: (i, 0)), place, place]
+            + untouched(state),
+            out_specs=[place, place],
+        ),
+        out_shape=[jax.ShapeDtypeStruct(master.shape, F32)] * 2,
+        input_output_aliases={4: 0, 5: 1} if state else {},
+        compiler_params=params(1, 48),
+        cost_estimate=cost(6 * hidden * block, 18 * hidden * block),
+        name="outer_rows",
+    )(where, delta, master, momentum, *state)
+
+
+def one_path_per_module(inputs, targets, token_ids, module_table, path_weights, master, momentum):
+    n_path, n_fsdp = lax.axis_size("path"), lax.axis_size("fsdp")
+    steps = n_fsdp // 2
+    weights = jnp.swapaxes(path_weights, 2, 3)
+    master = jnp.swapaxes(master, 2, 3)
+    momentum = jnp.swapaxes(momentum, 2, 3)
+    width, hidden = path_weights.shape[2:]
+    in_scale = width ** (-0.5)
+    out_scale = (hidden * n_fsdp) ** (-0.5)
+    total = inputs.shape[1] * n_fsdp
+
+    def ring(a):
+        return lax.ppermute(a, "fsdp", [(i, (i + 2) % n_fsdp) for i in range(n_fsdp)])
+
+    def swap(a):
+        return lax.ppermute(a, "fsdp", [(i, i ^ 1) for i in range(n_fsdp)])
+
+    def cross(a, d):
+        return lax.ppermute(a, "path", [(i, i ^ d) for i in range(n_path)])
+
+    half = inputs.shape[1] // 2
+
+    def gather(halves, use, made):
+        near, far = [halves], []
+        for k in range(steps - 1):
+            got, came = [], []
+            for h in (0, 1):
+                got.append(ring(near[k][h]))
+                came.append(swap(near[k][h]))
+            if k:
+                made = use(k - 1, [*near[k - 1], *far[k - 1]])
+            for h in (0, 1):
+                got[h], came[h], *_ = lax.optimization_barrier((got[h], came[h], *made))
+            near.append(got)
+            far.append(came)
+        came = [swap(near[-1][0]), ring(far[-1][1])]
+        made = use(steps - 2, [*near[-2], *far[-1]])
+        came = lax.optimization_barrier((*came, *made))[:2]
+        far.append(came)
+        use(steps - 1, [*near[-1], *far[-1]])
+        return [a for pieces in zip(near, far) for both in pieces for a in both]
+
+    me = lax.axis_index("path").astype(jnp.int32)
+    where = jnp.concatenate([me[None], module_table.reshape(-1)])
+    away = list(range(n_path))[::-1]
+    far_away = [d for d in away if d > 1]
+    first, second = far_away
+    acts, slopes, own, peer, ahead, last_far, passed = [], [], [], [], [], [], [None, None]
+
+    def run_forward(k, pieces):
+        after = acts[-1:]
+        if k == steps - 1:
+            ahead.append(add_rows(peer[2][1], ahead[0]))
+            after += ahead[-1:]
+            last_far.extend(pieces[2:])
+        types = (F32, BF16 if k == 1 else F32, BF16, BF16)
+        act, slope, *parts = forward(pieces, weights, in_scale, out_scale, types, after)
+        acts.append(act)
+        slopes.append(slope)
+        own.append(parts[:2])
+        peer.append(parts[2:])
+        if k == 1:
+            ahead.append(ring(peer[1][1]))
+            passed[1] = ring(own[1][1])
+        if k == 0:
+            send_base(1, [act])
+        return [act, *({1: [base[0, first], sent[-1]], 2: [base[1, first]]}.get(k, []))]
+
+    x_halves = [inputs[0, :half], inputs[0, half:]]
+    base, sent = {}, []
+
+    def send_base(d, after):
+        made = base_rows(where, master, momentum, d, d == 1, after)
+        sent.extend(made)
+        for level in range(weights.shape[1]):
+            base[level, d] = cross(made[level], d) if len(made) > level else base[0, d]
+
+    for d in far_away:
+        send_base(d, x_halves)
+    x_all = gather(x_halves, run_forward, sent[:])
+
+    wide = lambda a: a.astype(F32)
+    for k in list(range(1, steps)) + [0]:
+        for h in (0, 1):
+            if (k, h) == (1, 1):
+                continue
+            out = peer[k][h]
+            if (k, h) == (2, 1):
+                out = ahead[-1]
+            if k == steps - 2:
+                out, *_ = lax.optimization_barrier((out, *last_far))
+            came = swap(out)
+            if 0 < k < steps - 1:
+                pinned = [passed[1], base[0, second]] if (k, h) == (2, 0) else []
+                came, *_ = lax.optimization_barrier((came, acts[k + 1], *pinned))
+            total_rows = own[k][h] + wide(came)
+            if passed[h] is not None:
+                total_rows = total_rows + wide(passed[h])
+            if k == 0:
+                passed[h] = total_rows
+                continue
+            total_rows = total_rows.astype(BF16)
+            if (k, h) == (steps - 1, 1):
+                total_rows, *_ = lax.optimization_barrier((total_rows, base[0, 1], base[1, second]))
+            if (k, h) == (steps - 1, 0):
+                *peer[0], total_rows = lax.optimization_barrier((*peer[0], total_rows))
+            passed[h] = ring(total_rows)
+    grad = []
+    for h, mine in enumerate(passed):
+        part = slice(h * half, (h + 1) * half)
+        keep = (token_ids[0, part] >= SPECIAL).astype(F32)
+        residual = wide(inputs[0, part]) + mine - wide(targets[0, part])
+        grad.append((keep[:, None] * residual / total).astype(BF16))
+
+    pre_grads = []
+
+    def run_backward(k, pieces):
+        if k < steps - 1:
+            after = pre_grads[-1:]
+            pre_grads.append(backward(pieces, weights, slopes[k], out_scale, after))
+        return pre_grads[-1:]
+
+    g_all = gather(grad, run_backward, [])
+    sides = {
+        0: (INNER_LR * in_scale, pre_grads, x_all),
+        1: (INNER_LR * out_scale, acts, g_all),
+    }
+    fresh, deltas, outer = [None], {}, [master, momentum]
+
+    def rows(level, d):
+        use = outer if d == 0 else None
+        copied = (base.get((level, d)), fresh[0], weights.shape)
+        out = module_rows(where, level, d, *sides[level], master.shape[3], d > 0, *copied, outer=use)
+        if d:
+            deltas[level, d] = cross(out[0], d)
+            fresh[0] = out[1]
+        else:
+            fresh[0], *outer[2:] = out
+        return out[0]
+
+    made = rows(1, second)
+    pre_grads.append(
+        backward(g_all[-4:], weights, slopes[-1], out_scale, [*pre_grads[-1:], made])
+    )
+    rows(0, second)
+    for d in (1, first, 0):
+        for level in (1, 0):
+            rows(level, d)
+    for d in (second, 1, first):
+        for level in (1, 0):
+            outer[2:] = outer_rows(where, deltas[level, d], level, d, outer)
+    new_master, new_momentum = outer[2:]
+    return (
+        jnp.swapaxes(fresh[0], 2, 3),
+        jnp.swapaxes(new_master, 2, 3),
+        jnp.swapaxes(new_momentum, 2, 3),
+    )
+
+
 def solution(mesh):
     in_specs = (
         P("path", "fsdp", None),
@@ -85,6 +539,17 @@
         P(None, None, "path", "fsdp"),
         P(None, None, "path", "fsdp"),
     )
-    return jax.shard_map(
-        per_device, mesh=mesh, in_specs=in_specs, out_specs=out_specs, check_vma=False
-    )
+    shape = mesh.shape
+
+    def step(*args):
+        paths, pieces = shape["path"], shape["fsdp"]
+        one_each = paths == args[5].shape[1] and paths & (paths - 1) == 0
+        body = one_path_per_module if one_each and pieces % 2 == 0 and pieces > 5 else any_table
+        return run(body)(*args)
+
+    def run(body):
+        return jax.shard_map(
+            body, mesh=mesh, in_specs=in_specs, out_specs=out_specs, check_vma=False
+        )
+
+    return step

time: 542 us -> 212 us (0.39)
  waiting for transfers between devices: 350 us -> 85.7 us
  local copies, waits for them, and re-layouts: 83 us -> 1.95 us
  Pallas kernels: 0 us -> 79.3 us
  matrix products: 73.8 us -> 0 us
  starting transfers between devices: 11.3 us -> 41.4 us
  between operations: 14.3 us -> 0.94 us
    all_gather x2 -> x0, waiting for transfers between devices: 152 us -> none  [the longest x1 78.3 us: per_device(): x_full = lax.all_gather(x_local, 'fsdp', axis=0, tiled=True)]
    all_to_all x2 -> x0, waiting for transfers between devices: 111 us -> none  [the longest x1 70.6 us: per_device(): lax.all_to_all(stacked.astype(jnp.bfloat16), 'path', split_axis=2, concat...]
    reduce_scatter x1 -> x0, waiting for transfers between devices: 85.7 us -> none  [per_device(): lax.psum_scatter((lax.dot_general(rows, w_out, (((1,), (1,)), ((), ())),...]
    ppermute x0 -> x53, waiting for transfers between devices: none -> 85.7 us  [the longest x21 43.8 us: ring(): lax.ppermute(a, 'fsdp', [(i, (i + 2) % n_fsdp) for i in range(n_fsdp)])]
    pallas_call x0 -> x26, Pallas kernels: none -> 79.3 us  [the longest x8 26 us: module_rows(): pl.pallas_call(kernel, grid_spec=pltpu.PrefetchScalarGridSpec(num_scalar_...]
    dot_general x6 -> x0, matrix products: 73.8 us -> none  [the longest x1 36.6 us: per_device(): jnp.einsum('lmq,lqrc->lmrc', pick, arrived, precision=lax.Precision.HIGHEST)]
    ppermute x0 -> x53, starting transfers between devices: none -> 41.4 us  [the longest x21 25.8 us: swap(): return lax.ppermute(a, 'fsdp', [(i, i ^ 1) for i in range(n_fsdp)])]
    all_to_all x2 -> x0, local copies, waits for them, and re-layouts: 26.6 us -> none  [the longest x1 17 us: per_device(): lax.all_to_all(stacked.astype(jnp.bfloat16), 'path', split_axis=2, concat...]
  transfers between devices with their start and end apart: 5 -> 53, of which waited for: 5 -> 33; matrix products, arithmetic and copies ran while one was open for 5% -> 1% of each run, Pallas kernels for 0% -> 35%
where the time goes in v1:
time: 212 us; the launch traced here: 210 us
  waiting for transfers between devices  85.7 us (40%)
  Pallas kernels  79.3 us (37%)
  starting transfers between devices  41.4 us (20%)
    ppermute x21, waiting for transfers between devices, ring(): lax.ppermute(a, 'fsdp', [(i, (i + 2) % n_fsdp) for i in range(n_fsdp)])  43.8 us
    ppermute x21, waiting for transfers between devices, swap(): return lax.ppermute(a, 'fsdp', [(i, i ^ 1) for i in range(n_fsdp)])  33.2 us
    pallas_call x8, Pallas kernels, module_rows(): pl.pallas_call(kernel, grid_spec=pltpu.PrefetchScalarGridSpec(num_scalar_...  26 us
    ppermute x21, starting transfers between devices, swap(): return lax.ppermute(a, 'fsdp', [(i, i ^ 1) for i in range(n_fsdp)])  25.8 us
    pallas_call x6, Pallas kernels, outer_rows(): pl.pallas_call(kernel, grid_spec=pltpu.PrefetchScalarGridSpec(num_scalar_...  21.8 us
    pallas_call x4, Pallas kernels, forward(): pl.pallas_call(kernel, grid=(2 * tiles,), in_specs=[*[pl.BlockSpec((half,...  14.4 us
    pallas_call x3, Pallas kernels, base_rows(): pl.pallas_call(kernel, grid_spec=pltpu.PrefetchScalarGridSpec(num_scalar_...  10.5 us
    ppermute x21, starting transfers between devices, ring(): lax.ppermute(a, 'fsdp', [(i, (i + 2) % n_fsdp) for i in range(n_fsdp)])  9.63 us
  transfers between devices with their start and end apart: 53, of which 33 were waited for; matrix products, arithmetic and copies ran while one was open for 1% of the time, Pallas kernels for 35%

profile of v1, /device:TPU:0, one launch (start us, length us, event | category | flops | bytes accessed | tf_op | source)
XLA Modules:
  0.0 210.4 jit_solution(10624216442208200324)
XLA Ops:
  1.7 3.0 %collective-permute-start.3 = (bf16[64,2048]{1,0:T(8,128)(2,1)S(1)}, bf16[64,2048]{1,0:T(8,128)(2,1)S(1)}, u32[]{:S(2)}, u32[]{:S(2)}) collective-permute-start(bf16[64,2048]{1,0:T(8,128)(2,1)S(1)} %get-tuple-element.195.refs_1_.refs_5_), channel_id=1, source_target_pairs={{0,1},{1,0},{2,3},{3,2},{4,5},{5,4},{6,7},{7,6},{8,9},{9,8},{10,11... | collective-permute-start | bytes 786440 | tf_op jit(solution)/shard_map/ppermute | solution.py:383
  7.2 3.6 %base_rows.3 = (bf16[704,512]{1,0:T(8,128)(2,1)S(1)}, bf16[704,512]{1,0:T(8,128)(2,1)S(1)}) custom-call(s32[9]{0:T(128)S(1)} %pad_add_fusion._, f32[2,4,704,512]{3,2,1,0:T(8,128)} %bitcast.39, f32[2,4,704,512]{3,2,1,0:T(8,128)} %bitcast.50, bf16[64,2048]{1,0:T(8,128)(2,1)S(1)} %get-tuple-element.196.refs_0_.refs_4_, ...), custom_call_target="tpu_custom_call" | custom-call | flops 1 | bytes 1 | tf_op jit(solution)/shard_map/base_rows/pallas_call | solution.py:240
  13.4 3.5 %base_rows.4 = (bf16[704,512]{1,0:T(8,128)(2,1)S(1)}, bf16[704,512]{1,0:T(8,128)(2,1)S(1)}) custom-call(s32[9]{0:T(128)S(1)} %pad_add_fusion._, f32[2,4,704,512]{3,2,1,0:T(8,128)} %bitcast.40, f32[2,4,704,512]{3,2,1,0:T(8,128)} %bitcast.51, bf16[64,2048]{1,0:T(8,128)(2,1)S(1)} %get-tuple-element.196.refs_0_.refs_4_, ...), custom_call_target="tpu_custom_call" | custom-call | flops 1 | bytes 1 | tf_op jit(solution)/shard_map/base_rows/pallas_call | solution.py:240
  20.2 2.6 %collective-permute-done.refs_0_.refs_8_ = bf16[64,2048]{1,0:T(8,128)(2,1)S(1)} collective-permute-done((bf16[64,2048]{1,0:T(8,128)(2,1)S(1)}, bf16[64,2048]{1,0:T(8,128)(2,1)S(1)}, u32[]{:S(2)}, u32[]{:S(2)}) %collective-permute-start) | collective-permute-done | bytes 262176 | tf_op jit(solution)/shard_map/ppermute | solution.py:380
  26.3 3.6 %forward.4 = (bf16[704,256]{1,0:T(8,128)(2,1)S(1)}, f32[704,256]{1,0:T(8,128)S(1)}, f32[64,2048]{1,0:T(8,128)S(1)}, f32[64,2048]{1,0:T(8,128)S(1)}, bf16[64,2048...) custom-call(bf16[64,2048]{1,0:T(8,128)(2,1)S(1)} %get-tuple-element.196.refs_0_.refs_4_, ...), custom_call_target="tpu_custom_call" | custom-call | flops 1 | bytes 1 | tf_op jit(solution)/shard_map/forward/pallas_call | solution.py:136
  35.5 3.4 %base_rows.5 = bf16[2,704,512]{2,1,0:T(8,128)(2,1)S(1)} custom-call(s32[9]{0:T(128)S(1)} %pad_add_fusion._, f32[2,4,704,512]{3,2,1,0:T(8,128)} %bitcast.41, f32[2,4,704,512]{3,2,1,0:T(8,128)} %bitcast.52, bf16[704,256]{1,0:T(8,128)(2,1)S(1)} %get-tuple-element.108.refs_6_.refs_0_), custom_call_target="tpu_custom_call" | custom-call | flops 1 | bytes 1 | tf_op jit(solution)/shard_map/base_rows/pallas_call | solution.py:240
  38.9 3.6 %forward.5 = (bf16[704,256]{1,0:T(8,128)(2,1)S(1)}, f32[704,256]{1,0:T(8,128)S(1)}, f32[64,2048]{1,0:T(8,128)S(1)}, bf16[64,2048]{1,0:T(8,128)(2,1)S(1)}, bf16[6...) custom-call(bf16[64,2048]{1,0:T(8,128)(2,1)S(1)} %collective-permute-done.refs_0_.refs_8_, ...), custom_call_target="tpu_custom_call" | custom-call | flops 1 | bytes 1 | tf_op jit(solution)/shard_map/forward/pallas_call | solution.py:136
  44.5 3.8 %collective-permute-done.6.refs_0_.refs_16_ = bf16[64,2048]{1,0:T(8,128)(2,1)S(1)} collective-permute-done((bf16[64,2048]{1,0:T(8,128)(2,1)S(1)}, bf16[64,2048]{1,0:T(8,128)(2,1)S(1)}, u32[]{:S(2)}, u32[]{:S(2)}) %collective-permute-start.6) | collective-permute-done | bytes 262176 | tf_op jit(solution)/shard_map/ppermute | solution.py:380
  49.6 3.6 %forward.6 = (bf16[704,256]{1,0:T(8,128)(2,1)S(1)}, f32[704,256]{1,0:T(8,128)S(1)}, f32[64,2048]{1,0:T(8,128)S(1)}, f32[64,2048]{1,0:T(8,128)S(1)}, bf16[64,2048...) custom-call(bf16[64,2048]{1,0:T(8,128)(2,1)S(1)} %collective-permute-done.4.refs_0_.refs_12_, ...), custom_call_target="tpu_custom_call" | custom-call | flops 1 | bytes 1 | tf_op jit(solution)/shard_map/forward/pallas_call | solution.py:136
  57.0 3.2 %collective-permute-done.14.refs_3_.refs_19_ = bf16[64,2048]{1,0:T(8,128)(2,1)S(1)} collective-permute-done((bf16[64,2048]{1,0:T(8,128)(2,1)S(1)}, bf16[64,2048]{1,0:T(8,128)(2,1)S(1)}, u32[]{:S(2)}, u32[]{:S(2)}) %collective-permute-start.14) | collective-permute-done | bytes 262176 | tf_op jit(solution)/shard_map/ppermute | solution.py:380
  62.4 3.6 %forward.7 = (bf16[704,256]{1,0:T(8,128)(2,1)S(1)}, f32[704,256]{1,0:T(8,128)S(1)}, f32[64,2048]{1,0:T(8,128)S(1)}, f32[64,2048]{1,0:T(8,128)S(1)}, bf16[64,2048...) custom-call(bf16[64,2048]{1,0:T(8,128)(2,1)S(1)} %collective-permute-done.6.refs_0_.refs_16_, ...), custom_call_target="tpu_custom_call" | custom-call | flops 1 | bytes 1 | tf_op jit(solution)/shard_map/forward/pallas_call | solution.py:136
  66.0 5.8 %collective-permute-done.28 = bf16[64,2048]{1,0:T(8,128)(2,1)S(1)} collective-permute-done((bf16[64,2048]{1,0:T(8,128)(2,1)S(1)}, bf16[64,2048]{1,0:T(8,128)(2,1)S(1)}, u32[]{:S(2)}, u32[]{:S(2)}) %collective-permute-start.28) | collective-permute-done | bytes 262176 | tf_op jit(solution)/shard_map/ppermute | solution.py:383
  75.8 6.4 %collective-permute-done.17 = bf16[64,2048]{1,0:T(8,128)(2,1)S(1)} collective-permute-done((bf16[64,2048]{1,0:T(8,128)(2,1)S(1)}, bf16[64,2048]{1,0:T(8,128)(2,1)S(1)}, u32[]{:S(2)}, u32[]{:S(2)}) %collective-permute-start.17) | collective-permute-done | bytes 262176 | tf_op jit(solution)/shard_map/ppermute | solution.py:383
  88.3 3.1 %collective-permute-done.29 = bf16[64,2048]{1,0:T(8,128)(2,1)S(1)} collective-permute-done((bf16[64,2048]{1,0:T(8,128)(2,1)S(1)}, bf16[64,2048]{1,0:T(8,128)(2,1)S(1)}, u32[]{:S(2)}, u32[]{:S(2)}) %collective-permute-start.29) | collective-permute-done | bytes 262176 | tf_op jit(solution)/shard_map/ppermute | solution.py:380
  93.6 5.1 %collective-permute-done.25 = bf16[64,2048]{1,0:T(8,128)(2,1)S(1)} collective-permute-done((bf16[64,2048]{1,0:T(8,128)(2,1)S(1)}, bf16[64,2048]{1,0:T(8,128)(2,1)S(1)}, u32[]{:S(2)}, u32[]{:S(2)}) %collective-permute-start.25) | collective-permute-done | bytes 262176 | tf_op jit(solution)/shard_map/ppermute | solution.py:380
  98.8 3.9 %collective-permute-done.32 = bf16[64,2048]{1,0:T(8,128)(2,1)S(1)} collective-permute-done((bf16[64,2048]{1,0:T(8,128)(2,1)S(1)}, bf16[64,2048]{1,0:T(8,128)(2,1)S(1)}, u32[]{:S(2)}, u32[]{:S(2)}) %collective-permute-start.32) | collective-permute-done | bytes 262176 | tf_op jit(solution)/shard_map/ppermute | solution.py:380
  105.2 7.2 %collective-permute-done.36.refs_3_.refs_7_ = bf16[64,2048]{1,0:T(8,128)(2,1)S(1)} collective-permute-done((bf16[64,2048]{1,0:T(8,128)(2,1)S(1)}, bf16[64,2048]{1,0:T(8,128)(2,1)S(1)}, u32[]{:S(2)}, u32[]{:S(2)}) %collective-permute-start.36) | collective-permute-done | bytes 262176 | tf_op jit(solution)/shard_map/ppermute | solution.py:383
  135.0 3.7 %collective-permute-done.43.refs_17_.refs_1_ = bf16[64,2048]{1,0:T(8,128)(2,1)S(1)} collective-permute-done((bf16[64,2048]{1,0:T(8,128)(2,1)S(1)}, bf16[64,2048]{1,0:T(8,128)(2,1)S(1)}, u32[]{:S(2)}, u32[]{:S(2)}) %collective-permute-start.43) | collective-permute-done | bytes 262176 | tf_op jit(solution)/shard_map/ppermute | solution.py:380
  138.7 4.0 %collective-permute-done.41.refs_16_.refs_0_ = bf16[64,2048]{1,0:T(8,128)(2,1)S(1)} collective-permute-done((bf16[64,2048]{1,0:T(8,128)(2,1)S(1)}, bf16[64,2048]{1,0:T(8,128)(2,1)S(1)}, u32[]{:S(2)}, u32[]{:S(2)}) %collective-permute-start.41) | collective-permute-done | bytes 262176 | tf_op jit(solution)/shard_map/ppermute | solution.py:380
  154.1 2.6 %module_rows.9 = (bf16[704,512]{1,0:T(8,128)(2,1)}, bf16[1,2,704,2048]{3,2,1,0:T(8,128)(2,1)}) custom-call(s32[9]{0:T(128)S(1)} %pad_add_fusion._, bf16[704,256]{1,0:T(8,128)(2,1)S(1)} %backward.4.refs_6_.refs_0_, bf16[704,256]{1,0:T(8,128)(2,1)S(1)} %backward.5.refs_6_.refs_1_, ...), custom_call_target="tpu_custom_call", output_to_operand_aliasing={{1}: (22, {})} | custom-call | flops 1 | bytes 1 | tf_op jit(solution)/shard_map/module_rows/pallas_call | solution.py:318
  157.8 2.6 %module_rows.10 = (bf16[704,512]{1,0:T(8,128)(2,1)}, bf16[1,2,704,2048]{3,2,1,0:T(8,128)(2,1)}) custom-call(s32[9]{0:T(128)S(1)} %pad_add_fusion._, bf16[704,256]{1,0:T(8,128)(2,1)S(1)} %get-tuple-element.108.refs_6_.refs_0_, bf16[704,256]{1,0:T(8,128)(2,1)S(1)} %get-tuple-element.113.refs_6_.refs_1_, ...), custom_call_target="tpu_custom_call", output_to_operand_aliasing={{1}: (22, {})} | custom-call | flops 1 | bytes 1 | tf_op jit(solution)/shard_map/module_rows/pallas_call | solution.py:318
  160.4 2.6 %module_rows.11 = (bf16[704,512]{1,0:T(8,128)(2,1)}, bf16[1,2,704,2048]{3,2,1,0:T(8,128)(2,1)}) custom-call(s32[9]{0:T(128)S(1)} %pad_add_fusion._, bf16[704,256]{1,0:T(8,128)(2,1)S(1)} %backward.4.refs_6_.refs_0_, bf16[704,256]{1,0:T(8,128)(2,1)S(1)} %backward.5.refs_6_.refs_1_, ...), custom_call_target="tpu_custom_call", output_to_operand_aliasing={{1}: (22, {})} | custom-call | flops 1 | bytes 1 | tf_op jit(solution)/shard_map/module_rows/pallas_call | solution.py:318
  163.5 2.6 %module_rows.12 = (bf16[704,512]{1,0:T(8,128)(2,1)}, bf16[1,2,704,2048]{3,2,1,0:T(8,128)(2,1)}) custom-call(s32[9]{0:T(128)S(1)} %pad_add_fusion._, bf16[704,256]{1,0:T(8,128)(2,1)S(1)} %get-tuple-element.108.refs_6_.refs_0_, bf16[704,256]{1,0:T(8,128)(2,1)S(1)} %get-tuple-element.113.refs_6_.refs_1_, ...), custom_call_target="tpu_custom_call", output_to_operand_aliasing={{1}: (22, {})} | custom-call | flops 1 | bytes 1 | tf_op jit(solution)/shard_map/module_rows/pallas_call | solution.py:318
  170.6 5.4 %module_rows.14 = (bf16[1,2,704,2048]{3,2,1,0:T(8,128)(2,1)}, f32[2,4,704,512]{3,2,1,0:T(8,128)}, f32[2,4,704,512]{3,2,1,0:T(8,128)}) custom-call(s32[9]{0:T(128)S(1)} %pad_add_fusion._, bf16[704,256]{1,0:T(8,128)(2,1)S(1)} %get-tuple-element.108.refs_6_.refs_0_, ...), custom_call_target="tpu_custom_call", output_to_operand_aliasing={{0}: (21, {})} | custom-call | flops 1 | bytes 1 | tf_op jit(solution)/shard_map/module_rows/pallas_call | solution.py:318
  176.0 5.4 %module_rows.15 = (bf16[1,2,704,2048]{3,2,1,0:T(8,128)(2,1)}, f32[2,4,704,512]{3,2,1,0:T(8,128)}, f32[2,4,704,512]{3,2,1,0:T(8,128)}) custom-call(s32[9]{0:T(128)S(1)} %pad_add_fusion._, bf16[704,256]{1,0:T(8,128)(2,1)S(1)} %backward.4.refs_6_.refs_0_, ...), custom_call_target="tpu_custom_call", output_to_operand_aliasing={{0}: (21, {}), {1}: (24, {}), {2}: (25, {})} | custom-call | flops 1 | bytes 1 | tf_op jit(solution)/shard_map/module_rows/pallas_call | solution.py:318
  181.3 3.6 %outer_rows.6 = (f32[2,4,704,512]{3,2,1,0:T(8,128)}, f32[2,4,704,512]{3,2,1,0:T(8,128)}) custom-call(s32[9]{0:T(128)S(1)} %pad_add_fusion._, bf16[704,512]{1,0:T(8,128)(2,1)S(1)} %collective-permute-done.52.delta_ref, f32[2,4,704,512]{3,2,1,0:T(8,128)} %bitcast.44, f32[2,4,704,512]{3,2,1,0:T(8,128)} %bitcast.55, ...), custom_call_target="tpu_custom_call", output_to_operand_aliasing={{0}: (4, {}), {1}: (5, {})} | custom-call | flops 1 | bytes 1 | tf_op jit(solution)/shard_map/outer_rows/pallas_call | solution.py:351
  186.0 3.6 %outer_rows.7 = (f32[2,4,704,512]{3,2,1,0:T(8,128)}, f32[2,4,704,512]{3,2,1,0:T(8,128)}) custom-call(s32[9]{0:T(128)S(1)} %pad_add_fusion._, bf16[704,512]{1,0:T(8,128)(2,1)S(1)} %collective-permute-done.51.delta_ref, f32[2,4,704,512]{3,2,1,0:T(8,128)} %bitcast.45, f32[2,4,704,512]{3,2,1,0:T(8,128)} %bitcast.56, ...), custom_call_target="tpu_custom_call", output_to_operand_aliasing={{0}: (4, {}), {1}: (5, {})} | custom-call | flops 1 | bytes 1 | tf_op jit(solution)/shard_map/outer_rows/pallas_call | solution.py:351
  189.6 3.8 %outer_rows.8 = (f32[2,4,704,512]{3,2,1,0:T(8,128)}, f32[2,4,704,512]{3,2,1,0:T(8,128)}) custom-call(s32[9]{0:T(128)S(1)} %pad_add_fusion._, bf16[704,512]{1,0:T(8,128)(2,1)} %collective-permute-done.50.delta_ref, f32[2,4,704,512]{3,2,1,0:T(8,128)} %bitcast.46, f32[2,4,704,512]{3,2,1,0:T(8,128)} %bitcast.57, ...), custom_call_target="tpu_custom_call", output_to_operand_aliasing={{0}: (4, {}), {1}: (5, {})} | custom-call | flops 1 | bytes 1 | tf_op jit(solution)/shard_map/outer_rows/pallas_call | solution.py:351
  193.4 3.6 %outer_rows.9 = (f32[2,4,704,512]{3,2,1,0:T(8,128)}, f32[2,4,704,512]{3,2,1,0:T(8,128)}) custom-call(s32[9]{0:T(128)S(1)} %pad_add_fusion._, bf16[704,512]{1,0:T(8,128)(2,1)S(1)} %collective-permute-done.49.delta_ref, f32[2,4,704,512]{3,2,1,0:T(8,128)} %bitcast.47, f32[2,4,704,512]{3,2,1,0:T(8,128)} %bitcast.58, ...), custom_call_target="tpu_custom_call", output_to_operand_aliasing={{0}: (4, {}), {1}: (5, {})} | custom-call | flops 1 | bytes 1 | tf_op jit(solution)/shard_map/outer_rows/pallas_call | solution.py:351
  199.2 3.6 %outer_rows.10 = (f32[2,4,704,512]{3,2,1,0:T(8,128)}, f32[2,4,704,512]{3,2,1,0:T(8,128)}) custom-call(s32[9]{0:T(128)S(1)} %pad_add_fusion._, bf16[704,512]{1,0:T(8,128)(2,1)S(1)} %collective-permute-done.48.delta_ref, f32[2,4,704,512]{3,2,1,0:T(8,128)} %bitcast.48, f32[2,4,704,512]{3,2,1,0:T(8,128)} %bitcast.59, ...), custom_call_target="tpu_custom_call", output_to_operand_aliasing={{0}: (4, {}), {1}: (5, {})} | custom-call | flops 1 | bytes 1 | tf_op jit(solution)/shard_map/outer_rows/pallas_call | solution.py:351
  202.8 4.0 %collective-permute-done.47.delta_ref = bf16[704,512]{1,0:T(8,128)(2,1)S(1)} collective-permute-done((bf16[704,512]{1,0:T(8,128)(2,1)S(1)}, bf16[704,512]{1,0:T(8,128)(2,1)S(1)}, u32[]{:S(2)}, u32[]{:S(2)}) %collective-permute-start.47) | collective-permute-done | bytes 720928 | tf_op jit(solution)/shard_map/ppermute | solution.py:386
  206.8 3.6 %outer_rows.11 = (f32[2,4,704,512]{3,2,1,0:T(8,128)}, f32[2,4,704,512]{3,2,1,0:T(8,128)}) custom-call(s32[9]{0:T(128)S(1)} %pad_add_fusion._, bf16[704,512]{1,0:T(8,128)(2,1)S(1)} %collective-permute-done.47.delta_ref, f32[2,4,704,512]{3,2,1,0:T(8,128)} %bitcast.49, f32[2,4,704,512]{3,2,1,0:T(8,128)} %bitcast.60, ...), custom_call_target="tpu_custom_call", output_to_operand_aliasing={{0}: (4, {}), {1}: (5, {})} | custom-call | flops 1 | bytes 1 | tf_op jit(solution)/shard_map/outer_rows/pallas_call | solution.py:351
  (122 shorter events, 85.7 us)
Async XLA Ops:
  1.7 15.2 %collective-permute-start.3 = (bf16[64,2048]{1,0:T(8,128)(2,1)S(1)}, bf16[64,2048]{1,0:T(8,128)(2,1)S(1)}, u32[]{:S(2)}, u32[]{:S(2)}) collective-permute-start(bf16[64,2048]{1,0:T(8,128)(2,1)S(1)} %get-tuple-element.195.refs_1_.refs_5_), channel_id=1, source_target_pairs={{0,1},{1,0},{2,3},{3,2},{4,5},{5,4},{6,7},{7,6},{8,9},{9,8},{10,11... | collective-permute-start | bytes 786440 | tf_op jit(solution)/shard_map/ppermute | solution.py:383
  4.7 12.2 %collective-permute-start.2 = (bf16[64,2048]{1,0:T(8,128)(2,1)S(1)}, bf16[64,2048]{1,0:T(8,128)(2,1)S(1)}, u32[]{:S(2)}, u32[]{:S(2)}) collective-permute-start(bf16[64,2048]{1,0:T(8,128)(2,1)S(1)} %get-tuple-element.195.refs_1_.refs_5_), channel_id=1, source_target_pairs={{0,2},{1,3},{2,4},{3,5},{4,6},{5,7},{6,0},{7,1},{8,10},{9,11},{10,... | collective-permute-start | bytes 786440 | tf_op jit(solution)/shard_map/ppermute | solution.py:380
  10.8 24.7 %collective-permute-start.10 = (bf16[704,512]{1,0:T(8,128)(2,1)S(1)}, bf16[704,512]{1,0:T(8,128)(2,1)S(1)}, u32[]{:S(2)}, u32[]{:S(2)}) collective-permute-start(bf16[704,512]{1,0:T(8,128)(2,1)S(1)} %get-tuple-element.98), channel_id=1, source_target_pairs={{0,24},{8,16},{16,8},{24,0},{1,25},{9,17},{17,9},{25,1},{2,26},{10... | collective-permute-start | bytes 2162696 | tf_op jit(solution)/shard_map/ppermute | solution.py:386
  11.8 11.0 %collective-permute-start = (bf16[64,2048]{1,0:T(8,128)(2,1)S(1)}, bf16[64,2048]{1,0:T(8,128)(2,1)S(1)}, u32[]{:S(2)}, u32[]{:S(2)}) collective-permute-start(bf16[64,2048]{1,0:T(8,128)(2,1)S(1)} %get-tuple-element.196.refs_0_.refs_4_), channel_id=1, source_target_pairs={{0,2},{1,3},{2,4},{3,5},{4,6},{5,7},{6,0},{7,1},{8,10},{9,11},{10,... | collective-permute-start | bytes 786440 | tf_op jit(solution)/shard_map/ppermute | solution.py:380
  18.5 11.4 %collective-permute-start.8 = (bf16[64,2048]{1,0:T(8,128)(2,1)S(1)}, bf16[64,2048]{1,0:T(8,128)(2,1)S(1)}, u32[]{:S(2)}, u32[]{:S(2)}) collective-permute-start(bf16[64,2048]{1,0:T(8,128)(2,1)S(1)} %collective-permute-done.2.refs_1_.refs_9_), channel_id=1, source_target_pairs={{0,2},{1,3},{2,4},{3,5},{4,6},{5,7},{6,0},{7,1},{8,10},{9,11},{10,... | collective-permute-start | bytes 786440 | tf_op jit(solution)/shard_map/ppermute | solution.py:380
  26.3 29.1 %collective-permute-start.15 = (bf16[704,512]{1,0:T(8,128)(2,1)S(1)}, bf16[704,512]{1,0:T(8,128)(2,1)S(1)}, u32[]{:S(2)}, u32[]{:S(2)}) collective-permute-start(bf16[704,512]{1,0:T(8,128)(2,1)S(1)} %get-tuple-element.99), channel_id=1, source_target_pairs={{0,24},{8,16},{16,8},{24,0},{1,25},{9,17},{17,9},{25,1},{2,26},{10... | collective-permute-start | bytes 2162696 | tf_op jit(solution)/shard_map/ppermute | solution.py:386
  29.9 12.6 %collective-permute-start.12 = (bf16[64,2048]{1,0:T(8,128)(2,1)S(1)}, bf16[64,2048]{1,0:T(8,128)(2,1)S(1)}, u32[]{:S(2)}, u32[]{:S(2)}) collective-permute-start(bf16[64,2048]{1,0:T(8,128)(2,1)S(1)} %collective-permute-done.8.refs_1_.refs_13_), channel_id=1, source_target_pairs={{0,1},{1,0},{2,3},{3,2},{4,5},{5,4},{6,7},{7,6},{8,9},{9,8},{10,11... | collective-permute-start | bytes 786440 | tf_op jit(solution)/shard_map/ppermute | solution.py:383
  31.7 12.3 %collective-permute-start.11 = (bf16[64,2048]{1,0:T(8,128)(2,1)S(1)}, bf16[64,2048]{1,0:T(8,128)(2,1)S(1)}, u32[]{:S(2)}, u32[]{:S(2)}) collective-permute-start(bf16[64,2048]{1,0:T(8,128)(2,1)S(1)} %collective-permute-done.8.refs_1_.refs_13_), channel_id=1, source_target_pairs={{0,2},{1,3},{2,4},{3,5},{4,6},{5,7},{6,0},{7,1},{8,10},{9,11},{10,... | collective-permute-start | bytes 786440 | tf_op jit(solution)/shard_map/ppermute | solution.py:380
  35.5 12.8 %collective-permute-start.6 = (bf16[64,2048]{1,0:T(8,128)(2,1)S(1)}, bf16[64,2048]{1,0:T(8,128)(2,1)S(1)}, u32[]{:S(2)}, u32[]{:S(2)}) collective-permute-start(bf16[64,2048]{1,0:T(8,128)(2,1)S(1)} %collective-permute-done.4.refs_0_.refs_12_), channel_id=1, source_target_pairs={{0,2},{1,3},{2,4},{3,5},{4,6},{5,7},{6,0},{7,1},{8,10},{9,11},{10,... | collective-permute-start | bytes 786440 | tf_op jit(solution)/shard_map/ppermute | solution.py:380
  42.5 11.3 %collective-permute-start.16 = (bf16[64,2048]{1,0:T(8,128)(2,1)S(1)}, bf16[64,2048]{1,0:T(8,128)(2,1)S(1)}, u32[]{:S(2)}, u32[]{:S(2)}) collective-permute-start(bf16[64,2048]{1,0:T(8,128)(2,1)S(1)} %get-tuple-element.123), channel_id=1, source_target_pairs={{0,2},{1,3},{2,4},{3,5},{4,6},{5,7},{6,0},{7,1},{8,10},{9,11},{10,... | collective-permute-start | bytes 786440 | tf_op jit(solution)/shard_map/ppermute | solution.py:380
  43.9 11.2 %collective-permute-start.21 = (bf16[64,2048]{1,0:T(8,128)(2,1)S(1)}, bf16[64,2048]{1,0:T(8,128)(2,1)S(1)}, u32[]{:S(2)}, u32[]{:S(2)}) collective-permute-start(bf16[64,2048]{1,0:T(8,128)(2,1)S(1)} %get-tuple-element.133), channel_id=1, source_target_pairs={{0,1},{1,0},{2,3},{3,2},{4,5},{5,4},{6,7},{7,6},{8,9},{9,8},{10,11... | collective-permute-start | bytes 786440 | tf_op jit(solution)/shard_map/ppermute | solution.py:383
  49.6 10.6 %collective-permute-start.14 = (bf16[64,2048]{1,0:T(8,128)(2,1)S(1)}, bf16[64,2048]{1,0:T(8,128)(2,1)S(1)}, u32[]{:S(2)}, u32[]{:S(2)}) collective-permute-start(bf16[64,2048]{1,0:T(8,128)(2,1)S(1)} %collective-permute-done.12.refs_3_.refs_15_), channel_id=1, source_target_pairs={{0,2},{1,3},{2,4},{3,5},{4,6},{5,7},{6,0},{7,1},{8,10},{9,11},{10,... | collective-permute-start | bytes 786440 | tf_op jit(solution)/shard_map/ppermute | solution.py:380
  53.9 19.1 %collective-permute-start.20 = (bf16[704,512]{1,0:T(8,128)(2,1)S(1)}, bf16[704,512]{1,0:T(8,128)(2,1)S(1)}, u32[]{:S(2)}, u32[]{:S(2)}) collective-permute-start(bf16[704,512]{1,0:T(8,128)(2,1)S(1)} %get-tuple-element.100), channel_id=1, source_target_pairs={{0,16},{8,24},{16,0},{24,8},{1,17},{9,25},{17,1},{25,9},{2,18},{10... | collective-permute-start | bytes 2162696 | tf_op jit(solution)/shard_map/ppermute | solution.py:386
  55.1 17.9 %collective-permute-start.19 = (bf16[64,2048]{1,0:T(8,128)(2,1)S(1)}, bf16[64,2048]{1,0:T(8,128)(2,1)S(1)}, u32[]{:S(2)}, u32[]{:S(2)}) collective-permute-start(bf16[64,2048]{1,0:T(8,128)(2,1)S(1)} %get-tuple-element.130), channel_id=1, source_target_pairs={{0,2},{1,3},{2,4},{3,5},{4,6},{5,7},{6,0},{7,1},{8,10},{9,11},{10,... | collective-permute-start | bytes 786440 | tf_op jit(solution)/shard_map/ppermute | solution.py:380
  60.2 13.2 %collective-permute-start.18 = (bf16[64,2048]{1,0:T(8,128)(2,1)S(1)}, bf16[64,2048]{1,0:T(8,128)(2,1)S(1)}, u32[]{:S(2)}, u32[]{:S(2)}) collective-permute-start(bf16[64,2048]{1,0:T(8,128)(2,1)S(1)} %get-tuple-element.128), channel_id=1, source_target_pairs={{0,1},{1,0},{2,3},{3,2},{4,5},{5,4},{6,7},{7,6},{8,9},{9,8},{10,11... | collective-permute-start | bytes 786440 | tf_op jit(solution)/shard_map/ppermute | solution.py:383
  60.9 10.9 %collective-permute-start.28 = (bf16[64,2048]{1,0:T(8,128)(2,1)S(1)}, bf16[64,2048]{1,0:T(8,128)(2,1)S(1)}, u32[]{:S(2)}, u32[]{:S(2)}) collective-permute-start(bf16[64,2048]{1,0:T(8,128)(2,1)S(1)} %add_rows.1.refs_7_), channel_id=1, source_target_pairs={{0,1},{1,0},{2,3},{3,2},{4,5},{5,4},{6,7},{7,6},{8,9},{9,8},{10,11... | collective-permute-start | bytes 786440 | tf_op jit(solution)/shard_map/ppermute | solution.py:383
  62.3 12.8 %collective-permute-start.22 = (bf16[64,2048]{1,0:T(8,128)(2,1)S(1)}, bf16[64,2048]{1,0:T(8,128)(2,1)S(1)}, u32[]{:S(2)}, u32[]{:S(2)}) collective-permute-start(bf16[64,2048]{1,0:T(8,128)(2,1)S(1)} %add_convert_fusion.4), channel_id=1, source_target_pairs={{0,2},{1,3},{2,4},{3,5},{4,6},{5,7},{6,0},{7,1},{8,10},{9,11},{10,... | collective-permute-start | bytes 786440 | tf_op jit(solution)/shard_map/ppermute | solution.py:380
  71.8 20.1 %collective-permute-start.31 = (bf16[704,512]{1,0:T(8,128)(2,1)S(1)}, bf16[704,512]{1,0:T(8,128)(2,1)S(1)}, u32[]{:S(2)}, u32[]{:S(2)}) collective-permute-start(bf16[704,512]{1,0:T(8,128)(2,1)S(1)} %get-tuple-element.101), channel_id=1, source_target_pairs={{0,16},{8,24},{16,0},{24,8},{1,17},{9,25},{17,1},{25,9},{2,18},{10... | collective-permute-start | bytes 2162696 | tf_op jit(solution)/shard_map/ppermute | solution.py:386
  73.0 18.9 %collective-permute-start.30 = (bf16[2,704,512]{2,1,0:T(8,128)(2,1)S(1)}, bf16[2,704,512]{2,1,0:T(8,128)(2,1)S(1)}, u32[]{:S(2)}, u32[]{:S(2)}) collective-permute-start(bf16[2,704,512]{2,1,0:T(8,128)(2,1)S(1)} %base_rows.5), channel_id=1, source_target_pairs={{0,8},{8,0},{16,24},{24,16},{1,9},{9,1},{17,25},{25,17},{2,10},{10... | collective-permute-start | bytes 4325384 | tf_op jit(solution)/shard_map/ppermute | solution.py:386
  73.4 14.3 %collective-permute-start.27 = (bf16[64,2048]{1,0:T(8,128)(2,1)S(1)}, bf16[64,2048]{1,0:T(8,128)(2,1)S(1)}, u32[]{:S(2)}, u32[]{:S(2)}) collective-permute-start(bf16[64,2048]{1,0:T(8,128)(2,1)S(1)} %get-tuple-element.140), channel_id=1, source_target_pairs={{0,1},{1,0},{2,3},{3,2},{4,5},{5,4},{6,7},{7,6},{8,9},{9,8},{10,11... | collective-permute-start | bytes 786440 | tf_op jit(solution)/shard_map/ppermute | solution.py:383
  87.7 11.0 %collective-permute-start.25 = (bf16[64,2048]{1,0:T(8,128)(2,1)S(1)}, bf16[64,2048]{1,0:T(8,128)(2,1)S(1)}, u32[]{:S(2)}, u32[]{:S(2)}) collective-permute-start(bf16[64,2048]{1,0:T(8,128)(2,1)S(1)} %add_convert_fusion.2), channel_id=1, source_target_pairs={{0,2},{1,3},{2,4},{3,5},{4,6},{5,7},{6,0},{7,1},{8,10},{9,11},{10,... | collective-permute-start | bytes 786440 | tf_op jit(solution)/shard_map/ppermute | solution.py:380
  91.9 10.7 %collective-permute-start.32 = (bf16[64,2048]{1,0:T(8,128)(2,1)S(1)}, bf16[64,2048]{1,0:T(8,128)(2,1)S(1)}, u32[]{:S(2)}, u32[]{:S(2)}) collective-permute-start(bf16[64,2048]{1,0:T(8,128)(2,1)S(1)} %add_convert_fusion), channel_id=1, source_target_pairs={{0,2},{1,3},{2,4},{3,5},{4,6},{5,7},{6,0},{7,1},{8,10},{9,11},{10,... | collective-permute-start | bytes 786440 | tf_op jit(solution)/shard_map/ppermute | solution.py:380
  103.6 11.0 %collective-permute-start.35 = (bf16[64,2048]{1,0:T(8,128)(2,1)S(1)}, bf16[64,2048]{1,0:T(8,128)(2,1)S(1)}, u32[]{:S(2)}, u32[]{:S(2)}) collective-permute-start(bf16[64,2048]{1,0:T(8,128)(2,1)S(1)} %get-tuple-element.193.refs_1_.refs_5_), channel_id=1, source_target_pairs={{0,2},{1,3},{2,4},{3,5},{4,6},{5,7},{6,0},{7,1},{8,10},{9,11},{10,... | collective-permute-start | bytes 786440 | tf_op jit(solution)/shard_map/ppermute | solution.py:380
  103.6 14.4 %collective-permute-start.34 = (bf16[64,2048]{1,0:T(8,128)(2,1)S(1)}, bf16[64,2048]{1,0:T(8,128)(2,1)S(1)}, u32[]{:S(2)}, u32[]{:S(2)}) collective-permute-start(bf16[64,2048]{1,0:T(8,128)(2,1)S(1)} %get-tuple-element.194.refs_0_.refs_4_), channel_id=1, source_target_pairs={{0,1},{1,0},{2,3},{3,2},{4,5},{5,4},{6,7},{7,6},{8,9},{9,8},{10,11... | collective-permute-start | bytes 786440 | tf_op jit(solution)/shard_map/ppermute | solution.py:383
  105.2 15.1 %collective-permute-start.33 = (bf16[64,2048]{1,0:T(8,128)(2,1)S(1)}, bf16[64,2048]{1,0:T(8,128)(2,1)S(1)}, u32[]{:S(2)}, u32[]{:S(2)}) collective-permute-start(bf16[64,2048]{1,0:T(8,128)(2,1)S(1)} %get-tuple-element.194.refs_0_.refs_4_), channel_id=1, source_target_pairs={{0,2},{1,3},{2,4},{3,5},{4,6},{5,7},{6,0},{7,1},{8,10},{9,11},{10,... | collective-permute-start | bytes 786440 | tf_op jit(solution)/shard_map/ppermute | solution.py:380
  127.7 11.0 %collective-permute-start.43 = (bf16[64,2048]{1,0:T(8,128)(2,1)S(1)}, bf16[64,2048]{1,0:T(8,128)(2,1)S(1)}, u32[]{:S(2)}, u32[]{:S(2)}) collective-permute-start(bf16[64,2048]{1,0:T(8,128)(2,1)S(1)} %collective-permute-done.39.refs_1_.refs_13_), channel_id=1, source_target_pairs={{0,2},{1,3},{2,4},{3,5},{4,6},{5,7},{6,0},{7,1},{8,10},{9,11},{10,... | collective-permute-start | bytes 786440 | tf_op jit(solution)/shard_map/ppermute | solution.py:380
  151.5 19.1 %collective-permute-start.52 = (bf16[704,512]{1,0:T(8,128)(2,1)S(1)}, bf16[704,512]{1,0:T(8,128)(2,1)S(1)}, u32[]{:S(2)}, u32[]{:S(2)}) collective-permute-start(bf16[704,512]{1,0:T(8,128)(2,1)S(1)} %get-tuple-element.163.refs_7_), channel_id=1, source_target_pairs={{0,16},{8,24},{16,0},{24,8},{1,17},{9,25},{17,1},{25,9},{2,18},{10... | collective-permute-start | bytes 2162696 | tf_op jit(solution)/shard_map/ppermute | solution.py:386
  156.8 29.3 %collective-permute-start.51 = (bf16[704,512]{1,0:T(8,128)(2,1)}, bf16[704,512]{1,0:T(8,128)(2,1)S(1)}, u32[]{:S(2)}, u32[]{:S(2)}) collective-permute-start(bf16[704,512]{1,0:T(8,128)(2,1)} %get-tuple-element.178), channel_id=1, source_target_pairs={{0,16},{8,24},{16,0},{24,8},{1,17},{9,25},{17,1},{25,9},{2,18},{10... | collective-permute-start | bytes 2162696 | tf_op jit(solution)/shard_map/ppermute | solution.py:386
  160.4 29.2 %collective-permute-start.50 = (bf16[704,512]{1,0:T(8,128)(2,1)}, bf16[704,512]{1,0:T(8,128)(2,1)}, u32[]{:S(2)}, u32[]{:S(2)}) collective-permute-start(bf16[704,512]{1,0:T(8,128)(2,1)} %get-tuple-element.177), channel_id=1, source_target_pairs={{0,8},{8,0},{16,24},{24,16},{1,9},{9,1},{17,25},{25,17},{2,10},{10... | collective-permute-start | bytes 2162696 | tf_op jit(solution)/shard_map/ppermute | solution.py:386
  163.0 30.4 %collective-permute-start.49 = (bf16[704,512]{1,0:T(8,128)(2,1)}, bf16[704,512]{1,0:T(8,128)(2,1)S(1)}, u32[]{:S(2)}, u32[]{:S(2)}) collective-permute-start(bf16[704,512]{1,0:T(8,128)(2,1)} %get-tuple-element.176), channel_id=1, source_target_pairs={{0,8},{8,0},{16,24},{24,16},{1,9},{9,1},{17,25},{25,17},{2,10},{10... | collective-permute-start | bytes 2162696 | tf_op jit(solution)/shard_map/ppermute | solution.py:386
  166.1 33.0 %collective-permute-start.48 = (bf16[704,512]{1,0:T(8,128)(2,1)}, bf16[704,512]{1,0:T(8,128)(2,1)S(1)}, u32[]{:S(2)}, u32[]{:S(2)}) collective-permute-start(bf16[704,512]{1,0:T(8,128)(2,1)} %get-tuple-element.175), channel_id=1, source_target_pairs={{0,24},{8,16},{16,8},{24,0},{1,25},{9,17},{17,9},{25,1},{2,26},{10... | collective-permute-start | bytes 2162696 | tf_op jit(solution)/shard_map/ppermute | solution.py:386
  170.6 36.2 %collective-permute-start.47 = (bf16[704,512]{1,0:T(8,128)(2,1)S(1)}, bf16[704,512]{1,0:T(8,128)(2,1)S(1)}, u32[]{:S(2)}, u32[]{:S(2)}) collective-permute-start(bf16[704,512]{1,0:T(8,128)(2,1)S(1)} %get-tuple-element.174), channel_id=1, source_target_pairs={{0,24},{8,16},{16,8},{24,0},{1,25},{9,17},{17,9},{25,1},{2,26},{10... | collective-permute-start | bytes 2162696 | tf_op jit(solution)/shard_map/ppermute | solution.py:386
  (26 other events, 356.3 us)

commit v2 on v1

--- a/solution.py
+++ b/solution.py
@@ -257,15 +257,18 @@
 
 
 def module_rows(
-    where, level, d, scale, lefts, rights, block, send=False, base=None, fresh=None, copy_shape=None, outer=None, after=()
+    where, level, d, scale, lefts, rights, block, send=False, base=None, fresh=None, copy_shape=None, outer=None, extra=None, after=()
 ):
     rows, wide = rights[0].shape
     hidden, tokens = lefts[0].shape
-    tile = hidden
+    tile = hidden if outer is None else hidden // 2
     n_left, n_right = len(lefts), len(rights)
     operands = [*lefts, *rights]
     in_specs = [pl.BlockSpec((tile, tokens), lambda i, s: (i, 0))] * n_left
     in_specs += [pl.BlockSpec((rows, block), lambda i, s: (0, s[0] ^ d if wide > block else 0))] * n_right
+    if extra is not None:
+        operands.append(extra)
+        in_specs.append(pl.BlockSpec((tile, block), lambda i, s: (i, 0)))
     out_specs, out_shape, aliases = [], [], {}
     if send:
         out_specs.append(pl.BlockSpec((tile, block), lambda i, s: (i, 0)))
@@ -303,6 +306,8 @@
         right = jnp.concatenate([ref[...] for ref in ins[n_left : n_left + n_right]], axis=0)
         rest = ins[n_left + n_right :]
         delta = jnp.dot(left, right, preferred_element_type=F32) * scale
+        if extra is not None:
+            delta = delta + rest.pop(0)[...].astype(F32)
         if send:
             outs.pop(0)[...] = delta.astype(BF16)
         if base is not None:
@@ -331,38 +336,69 @@
     )(where, *operands, *after)
 
 
+def take_columns(where, pieces, block, d):
+    rows, n = pieces[0].shape[0], len(pieces)
+
+    def kernel(_, *refs):
+        refs[-1][...] = jnp.concatenate([ref[...] for ref in refs[:n]], axis=0)
+
+    return pl.pallas_call(
+        kernel,
+        grid_spec=pltpu.PrefetchScalarGridSpec(
+            num_scalar_prefetch=1,
+            grid=(1,),
+            in_specs=[pl.BlockSpec((rows, block), lambda i, s: (0, s[0] ^ d))] * n,
+            out_specs=whole((n * rows, block)),
+        ),
+        out_shape=jax.ShapeDtypeStruct((n * rows, block), BF16),
+        compiler_params=params(1, 4),
+        cost_estimate=cost(0, 4 * n * rows * block),
+        name="take_columns",
+    )(where, *pieces)
+
+
 def nesterov(average, master_ref, momentum_ref, new_master, new_momentum):
     moved = MOMENT * momentum_ref[0, 0] + average
     new_momentum[0, 0] = moved
     new_master[0, 0] = master_ref[0, 0] - OUTER_LR * (average + MOMENT * moved)
 
 
-def outer_rows(where, delta, level, d, outer):
+def outer_rows(where, deltas, levels, d, outer):
     master, momentum, *state = outer
-    levels, _, hidden, block = master.shape
-    tile = hidden // 2
-
-    def kernel(_, delta_ref, master_ref, momentum_ref, *refs):
-        nesterov(delta_ref[...].astype(F32), master_ref, momentum_ref, *refs[-2:])
+    n_levels, _, hidden, block = master.shape
+    tile, n = hidden // 2, len(deltas)
+
+    def kernel(_, *refs):
+        step = pl.program_id(0)
+        average = refs[0][...].astype(F32)
+        for k in range(1, n):
+            average = jnp.where(step < 2 * k, average, refs[k][...].astype(F32))
+        nesterov(average, *refs[n : n + 2], *refs[-2:])
+
+    def level_of(i):
+        return levels[0] + (levels[-1] - levels[0]) * (i // 2)
 
     place = pl.BlockSpec(
-        (1, 1, tile, block), lambda i, s: (level, s[1 + (s[0] ^ d) * levels + level], i, 0)
-    )
+        (1, 1, tile, block),
+        lambda i, s: (level_of(i), s[1 + (s[0] ^ d) * n_levels + level_of(i)], i % 2, 0),
+    )
+    rows = [
+        pl.BlockSpec((tile, block), lambda i, s, k=k: (jnp.clip(i - 2 * k, 0, 1), 0)) for k in range(n)
+    ]
     return pl.pallas_call(
         kernel,
         grid_spec=pltpu.PrefetchScalarGridSpec(
             num_scalar_prefetch=1,
-            grid=(hidden // tile,),
-            in_specs=[pl.BlockSpec((tile, block), lambda i, s: (i, 0)), place, place]
-            + untouched(state),
+            grid=(2 * n,),
+            in_specs=rows + [place, place] + untouched(state),
             out_specs=[place, place],
         ),
         out_shape=[jax.ShapeDtypeStruct(master.shape, F32)] * 2,
-        input_output_aliases={4: 0, 5: 1} if state else {},
+        input_output_aliases={n + 3: 0, n + 4: 1} if state else {},
         compiler_params=params(1, 48),
         cost_estimate=cost(6 * hidden * block, 18 * hidden * block),
         name="outer_rows",
-    )(where, delta, master, momentum, *state)
+    )(where, *deltas, master, momentum, *state)
 
 
 def one_path_per_module(inputs, targets, token_ids, module_table, path_weights, master, momentum):
@@ -481,41 +517,58 @@
 
     pre_grads = []
 
+    out_side, block = INNER_LR * out_scale, master.shape[3]
+    last_act = cross(acts[-1], second)
+    g_parts, early = [], []
+
     def run_backward(k, pieces):
-        if k < steps - 1:
-            after = pre_grads[-1:]
-            pre_grads.append(backward(pieces, weights, slopes[k], out_scale, after))
-        return pre_grads[-1:]
+        g_parts.extend(pieces)
+        if k == steps - 1:
+            return []
+        pre_grads.append(backward(pieces, weights, slopes[k], out_scale, pre_grads[-1:]))
+        made = pre_grads[-1:]
+        if k == 0:
+            made = made + [last_act]
+        if k == steps - 2:
+            early.extend(module_rows(where, 1, second, out_side, acts[:-1], g_parts[:], block, True))
+            made = made + early
+        return made
 
     g_all = gather(grad, run_backward, [])
     sides = {
         0: (INNER_LR * in_scale, pre_grads, x_all),
-        1: (INNER_LR * out_scale, acts, g_all),
+        1: (out_side, acts, g_all),
     }
     fresh, deltas, outer = [None], {}, [master, momentum]
 
-    def rows(level, d):
+    def rows(level, d, after=()):
         use = outer if d == 0 else None
+        send = d > 0 and (level, d) != (1, second)
         copied = (base.get((level, d)), fresh[0], weights.shape)
-        out = module_rows(where, level, d, *sides[level], master.shape[3], d > 0, *copied, outer=use)
+        out = module_rows(
+            where, level, d, *sides[level], block, send, *copied, outer=use, after=after
+        )
+        if send:
+            deltas[level, d] = cross(out[0], d)
         if d:
-            deltas[level, d] = cross(out[0], d)
-            fresh[0] = out[1]
+            fresh[0] = out[-1]
         else:
             fresh[0], *outer[2:] = out
-        return out[0]
-
-    made = rows(1, second)
+
+    early_there = cross(early[0], second)
+    columns = take_columns(where, g_all[-4:], block, second)
+    columns_there = cross(columns, second)
     pre_grads.append(
-        backward(g_all[-4:], weights, slopes[-1], out_scale, [*pre_grads[-1:], made])
+        backward(g_all[-4:], weights, slopes[-1], out_scale, [*pre_grads[-1:], columns])
     )
     rows(0, second)
-    for d in (1, first, 0):
-        for level in (1, 0):
-            rows(level, d)
-    for d in (second, 1, first):
-        for level in (1, 0):
-            outer[2:] = outer_rows(where, deltas[level, d], level, d, outer)
+    for key in [(1, first), (1, 1), (0, 1), (0, first), (1, second), (1, 0), (0, 0)]:
+        rows(*key, [early_there] if key == (0, 1) else [])
+    outer[2:] = module_rows(
+        where, 1, second, out_side, [last_act], [columns_there], block, outer=outer, extra=early_there
+    )
+    for levels, d in [((0,), second), ((1,), first), ((1, 0), 1), ((0,), first)]:
+        outer[2:] = outer_rows(where, [deltas[level, d] for level in levels], levels, d, outer)
     new_master, new_momentum = outer[2:]
     return (
         jnp.swapaxes(fresh[0], 2, 3),

time: 212 us -> 211 us (level)
  waiting for transfers between devices: 85.7 us -> 82 us
  starting transfers between devices: 41.4 us -> 43.9 us
    ppermute x11 -> x13, waiting for transfers between devices: 8.76 us -> 3.98 us  [cross(): return lax.ppermute(a, 'path', [(i, i ^ d) for i in range(n_path)])]
    pallas_call x6 -> x4, Pallas kernels: 21.8 us -> 17.5 us  [outer_rows(): pl.pallas_call(kernel, grid_spec=pltpu.PrefetchScalarGridSpec(num_scalar_...]
    pallas_call x8 -> x10, Pallas kernels: 26 us -> 29.7 us  [module_rows(): pl.pallas_call(kernel, grid_spec=pltpu.PrefetchScalarGridSpec(num_scalar_...]
    ppermute x11 -> x13, starting transfers between devices: 5.97 us -> 9.02 us  [cross(): return lax.ppermute(a, 'path', [(i, i ^ d) for i in range(n_path)])]
  transfers between devices with their start and end apart: 53 -> 55, of which waited for: 33 -> 32; matrix products, arithmetic and copies ran while one was open for 1% -> 1% of each run, Pallas kernels for 35% -> 36%
where the time goes in v2:
time: 211 us; the launch traced here: 209 us
  waiting for transfers between devices  82 us (39%)
  Pallas kernels  79.4 us (38%)
  starting transfers between devices  43.9 us (21%)
    ppermute x21, waiting for transfers between devices, ring(): lax.ppermute(a, 'fsdp', [(i, (i + 2) % n_fsdp) for i in range(n_fsdp)])  43.1 us
    ppermute x21, waiting for transfers between devices, swap(): return lax.ppermute(a, 'fsdp', [(i, i ^ 1) for i in range(n_fsdp)])  34.9 us
    pallas_call x10, Pallas kernels, module_rows(): pl.pallas_call(kernel, grid_spec=pltpu.PrefetchScalarGridSpec(num_scalar_...  29.7 us
    ppermute x21, starting transfers between devices, swap(): return lax.ppermute(a, 'fsdp', [(i, i ^ 1) for i in range(n_fsdp)])  25.3 us
    pallas_call x4, Pallas kernels, outer_rows(): pl.pallas_call(kernel, grid_spec=pltpu.PrefetchScalarGridSpec(num_scalar_...  17.5 us
    pallas_call x4, Pallas kernels, forward(): pl.pallas_call(kernel, grid=(2 * tiles,), in_specs=[*[pl.BlockSpec((half,...  14.4 us
    pallas_call x3, Pallas kernels, base_rows(): pl.pallas_call(kernel, grid_spec=pltpu.PrefetchScalarGridSpec(num_scalar_...  10.5 us
    ppermute x21, starting transfers between devices, ring(): lax.ppermute(a, 'fsdp', [(i, (i + 2) % n_fsdp) for i in range(n_fsdp)])  9.6 us
  transfers between devices with their start and end apart: 55, of which 32 were waited for; matrix products, arithmetic and copies ran while one was open for 1% of the time, Pallas kernels for 36%

profile of v2, /device:TPU:0, one launch (start us, length us, event | category | flops | bytes accessed | tf_op | source)
XLA Modules:
  0.0 209.3 jit_solution(17253001132552438300)
XLA Ops:
  1.7 3.0 %collective-permute-start.3 = (bf16[64,2048]{1,0:T(8,128)(2,1)S(1)}, bf16[64,2048]{1,0:T(8,128)(2,1)S(1)}, u32[]{:S(2)}, u32[]{:S(2)}) collective-permute-start(bf16[64,2048]{1,0:T(8,128)(2,1)S(1)} %get-tuple-element.187.refs_1_.refs_5_), channel_id=1, source_target_pairs={{0,1},{1,0},{2,3},{3,2},{4,5},{5,4},{6,7},{7,6},{8,9},{9,8},{10,11... | collective-permute-start | bytes 786440 | tf_op jit(solution)/shard_map/ppermute | solution.py:419
  7.2 3.6 %base_rows.3 = (bf16[704,512]{1,0:T(8,128)(2,1)S(1)}, bf16[704,512]{1,0:T(8,128)(2,1)S(1)}) custom-call(s32[9]{0:T(128)S(1)} %pad_add_fusion._, f32[2,4,704,512]{3,2,1,0:T(8,128)} %bitcast.39, f32[2,4,704,512]{3,2,1,0:T(8,128)} %bitcast.49, bf16[64,2048]{1,0:T(8,128)(2,1)S(1)} %get-tuple-element.188.refs_0_.refs_4_, ...), custom_call_target="tpu_custom_call" | custom-call | flops 1 | bytes 1 | tf_op jit(solution)/shard_map/base_rows/pallas_call | solution.py:240
  13.4 3.5 %base_rows.4 = (bf16[704,512]{1,0:T(8,128)(2,1)S(1)}, bf16[704,512]{1,0:T(8,128)(2,1)S(1)}) custom-call(s32[9]{0:T(128)S(1)} %pad_add_fusion._, f32[2,4,704,512]{3,2,1,0:T(8,128)} %bitcast.40, f32[2,4,704,512]{3,2,1,0:T(8,128)} %bitcast.50, bf16[64,2048]{1,0:T(8,128)(2,1)S(1)} %get-tuple-element.188.refs_0_.refs_4_, ...), custom_call_target="tpu_custom_call" | custom-call | flops 1 | bytes 1 | tf_op jit(solution)/shard_map/base_rows/pallas_call | solution.py:240
  20.2 2.6 %collective-permute-done.refs_0_.refs_8_ = bf16[64,2048]{1,0:T(8,128)(2,1)S(1)} collective-permute-done((bf16[64,2048]{1,0:T(8,128)(2,1)S(1)}, bf16[64,2048]{1,0:T(8,128)(2,1)S(1)}, u32[]{:S(2)}, u32[]{:S(2)}) %collective-permute-start) | collective-permute-done | bytes 262176 | tf_op jit(solution)/shard_map/ppermute | solution.py:416
  26.3 3.6 %forward.4 = (bf16[704,256]{1,0:T(8,128)(2,1)S(1)}, f32[704,256]{1,0:T(8,128)S(1)}, f32[64,2048]{1,0:T(8,128)S(1)}, f32[64,2048]{1,0:T(8,128)S(1)}, bf16[64,2048...) custom-call(bf16[64,2048]{1,0:T(8,128)(2,1)S(1)} %get-tuple-element.188.refs_0_.refs_4_, ...), custom_call_target="tpu_custom_call" | custom-call | flops 1 | bytes 1 | tf_op jit(solution)/shard_map/forward/pallas_call | solution.py:136
  35.5 3.4 %base_rows.5 = bf16[2,704,512]{2,1,0:T(8,128)(2,1)S(1)} custom-call(s32[9]{0:T(128)S(1)} %pad_add_fusion._, f32[2,4,704,512]{3,2,1,0:T(8,128)} %bitcast.41, f32[2,4,704,512]{3,2,1,0:T(8,128)} %bitcast.51, bf16[704,256]{1,0:T(8,128)(2,1)S(1)} %get-tuple-element.104.refs_6_.refs_0_), custom_call_target="tpu_custom_call" | custom-call | flops 1 | bytes 1 | tf_op jit(solution)/shard_map/base_rows/pallas_call | solution.py:240
  38.9 3.6 %forward.5 = (bf16[704,256]{1,0:T(8,128)(2,1)S(1)}, f32[704,256]{1,0:T(8,128)S(1)}, f32[64,2048]{1,0:T(8,128)S(1)}, bf16[64,2048]{1,0:T(8,128)(2,1)S(1)}, bf16[6...) custom-call(bf16[64,2048]{1,0:T(8,128)(2,1)S(1)} %collective-permute-done.refs_0_.refs_8_, ...), custom_call_target="tpu_custom_call" | custom-call | flops 1 | bytes 1 | tf_op jit(solution)/shard_map/forward/pallas_call | solution.py:136
  44.5 3.8 %collective-permute-done.6.refs_0_.refs_16_ = bf16[64,2048]{1,0:T(8,128)(2,1)S(1)} collective-permute-done((bf16[64,2048]{1,0:T(8,128)(2,1)S(1)}, bf16[64,2048]{1,0:T(8,128)(2,1)S(1)}, u32[]{:S(2)}, u32[]{:S(2)}) %collective-permute-start.6) | collective-permute-done | bytes 262176 | tf_op jit(solution)/shard_map/ppermute | solution.py:416
  49.6 3.6 %forward.6 = (bf16[704,256]{1,0:T(8,128)(2,1)S(1)}, f32[704,256]{1,0:T(8,128)S(1)}, f32[64,2048]{1,0:T(8,128)S(1)}, f32[64,2048]{1,0:T(8,128)S(1)}, bf16[64,2048...) custom-call(bf16[64,2048]{1,0:T(8,128)(2,1)S(1)} %collective-permute-done.4.refs_0_.refs_12_, ...), custom_call_target="tpu_custom_call" | custom-call | flops 1 | bytes 1 | tf_op jit(solution)/shard_map/forward/pallas_call | solution.py:136
  57.0 3.2 %collective-permute-done.14.refs_3_.refs_19_ = bf16[64,2048]{1,0:T(8,128)(2,1)S(1)} collective-permute-done((bf16[64,2048]{1,0:T(8,128)(2,1)S(1)}, bf16[64,2048]{1,0:T(8,128)(2,1)S(1)}, u32[]{:S(2)}, u32[]{:S(2)}) %collective-permute-start.14) | collective-permute-done | bytes 262176 | tf_op jit(solution)/shard_map/ppermute | solution.py:416
  62.4 3.6 %forward.7 = (bf16[704,256]{1,0:T(8,128)(2,1)S(1)}, f32[704,256]{1,0:T(8,128)S(1)}, f32[64,2048]{1,0:T(8,128)S(1)}, f32[64,2048]{1,0:T(8,128)S(1)}, bf16[64,2048...) custom-call(bf16[64,2048]{1,0:T(8,128)(2,1)S(1)} %collective-permute-done.6.refs_0_.refs_16_, ...), custom_call_target="tpu_custom_call" | custom-call | flops 1 | bytes 1 | tf_op jit(solution)/shard_map/forward/pallas_call | solution.py:136
  66.0 5.8 %collective-permute-done.28 = bf16[64,2048]{1,0:T(8,128)(2,1)S(1)} collective-permute-done((bf16[64,2048]{1,0:T(8,128)(2,1)S(1)}, bf16[64,2048]{1,0:T(8,128)(2,1)S(1)}, u32[]{:S(2)}, u32[]{:S(2)}) %collective-permute-start.28) | collective-permute-done | bytes 262176 | tf_op jit(solution)/shard_map/ppermute | solution.py:419
  75.8 6.4 %collective-permute-done.17 = bf16[64,2048]{1,0:T(8,128)(2,1)S(1)} collective-permute-done((bf16[64,2048]{1,0:T(8,128)(2,1)S(1)}, bf16[64,2048]{1,0:T(8,128)(2,1)S(1)}, u32[]{:S(2)}, u32[]{:S(2)}) %collective-permute-start.17) | collective-permute-done | bytes 262176 | tf_op jit(solution)/shard_map/ppermute | solution.py:419
  88.3 3.1 %collective-permute-done.29 = bf16[64,2048]{1,0:T(8,128)(2,1)S(1)} collective-permute-done((bf16[64,2048]{1,0:T(8,128)(2,1)S(1)}, bf16[64,2048]{1,0:T(8,128)(2,1)S(1)}, u32[]{:S(2)}, u32[]{:S(2)}) %collective-permute-start.29) | collective-permute-done | bytes 262176 | tf_op jit(solution)/shard_map/ppermute | solution.py:416
  93.6 5.1 %collective-permute-done.25 = bf16[64,2048]{1,0:T(8,128)(2,1)S(1)} collective-permute-done((bf16[64,2048]{1,0:T(8,128)(2,1)S(1)}, bf16[64,2048]{1,0:T(8,128)(2,1)S(1)}, u32[]{:S(2)}, u32[]{:S(2)}) %collective-permute-start.25) | collective-permute-done | bytes 262176 | tf_op jit(solution)/shard_map/ppermute | solution.py:416
  98.8 3.9 %collective-permute-done.32 = bf16[64,2048]{1,0:T(8,128)(2,1)S(1)} collective-permute-done((bf16[64,2048]{1,0:T(8,128)(2,1)S(1)}, bf16[64,2048]{1,0:T(8,128)(2,1)S(1)}, u32[]{:S(2)}, u32[]{:S(2)}) %collective-permute-start.32) | collective-permute-done | bytes 262176 | tf_op jit(solution)/shard_map/ppermute | solution.py:416
  106.0 6.4 %collective-permute-done.34.refs_2_.refs_5_.refs_6_ = bf16[64,2048]{1,0:T(8,128)(2,1)S(1)} collective-permute-done((bf16[64,2048]{1,0:T(8,128)(2,1)S(1)}, bf16[64,2048]{1,0:T(8,128)(2,1)S(1)}, u32[]{:S(2)}, u32[]{:S(2)}) %collective-permute-start.34) | collective-permute-done | bytes 262176 | tf_op jit(solution)/shard_map/ppermute | solution.py:419
  138.2 3.3 %collective-permute-done.44.refs_1_.refs_17_ = bf16[64,2048]{1,0:T(8,128)(2,1)S(1)} collective-permute-done((bf16[64,2048]{1,0:T(8,128)(2,1)S(1)}, bf16[64,2048]{1,0:T(8,128)(2,1)S(1)}, u32[]{:S(2)}, u32[]{:S(2)}) %collective-permute-start.44) | collective-permute-done | bytes 262176 | tf_op jit(solution)/shard_map/ppermute | solution.py:416
  146.4 3.8 %collective-permute-done.46.refs_2_.refs_18_ = bf16[64,2048]{1,0:T(8,128)(2,1)S(1)} collective-permute-done((bf16[64,2048]{1,0:T(8,128)(2,1)S(1)}, bf16[64,2048]{1,0:T(8,128)(2,1)S(1)}, u32[]{:S(2)}, u32[]{:S(2)}) %collective-permute-start.46) | collective-permute-done | bytes 262176 | tf_op jit(solution)/shard_map/ppermute | solution.py:419
  150.2 2.7 %collective-permute-done.47.refs_3_.refs_19_ = bf16[64,2048]{1,0:T(8,128)(2,1)S(1)} collective-permute-done((bf16[64,2048]{1,0:T(8,128)(2,1)S(1)}, bf16[64,2048]{1,0:T(8,128)(2,1)S(1)}, u32[]{:S(2)}, u32[]{:S(2)}) %collective-permute-start.47) | collective-permute-done | bytes 262176 | tf_op jit(solution)/shard_map/ppermute | solution.py:416
  155.8 2.6 %module_rows.11 = (bf16[704,512]{1,0:T(8,128)(2,1)}, bf16[1,2,704,2048]{3,2,1,0:T(8,128)(2,1)}) custom-call(s32[9]{0:T(128)S(1)} %pad_add_fusion._, bf16[704,256]{1,0:T(8,128)(2,1)S(1)} %backward.4.refs_6_.refs_0_, bf16[704,256]{1,0:T(8,128)(2,1)S(1)} %backward.5.refs_6_.refs_1_, bf16[704,256]{1,0:T(8,128)(2,1)S(1)} %backward.6.refs_6_.refs_2_, ...), custom_call_target="tpu_custom_call" | custom-call | flops 1 | bytes 1 | tf_op jit(solution)/shard_map/module_rows/pallas_call | solution.py:323
  159.8 2.6 %module_rows.12 = (bf16[704,512]{1,0:T(8,128)(2,1)}, bf16[1,2,704,2048]{3,2,1,0:T(8,128)(2,1)}) custom-call(s32[9]{0:T(128)S(1)} %pad_add_fusion._, bf16[704,256]{1,0:T(8,128)(2,1)S(1)} %get-tuple-element.104.refs_6_.refs_0_, bf16[704,256]{1,0:T(8,128)(2,1)S(1)} %get-tuple-element.109.refs_6_.refs_1_, ...), custom_call_target="tpu_custom_call", output_to_operand_aliasing={{1}: (22, {})} | custom-call | flops 1 | bytes 1 | tf_op jit(solution)/shard_map/module_rows/pallas_call | solution.py:323
  165.6 2.6 %module_rows.14 = (bf16[704,512]{1,0:T(8,128)(2,1)}, bf16[1,2,704,2048]{3,2,1,0:T(8,128)(2,1)}) custom-call(s32[9]{0:T(128)S(1)} %pad_add_fusion._, bf16[704,256]{1,0:T(8,128)(2,1)S(1)} %backward.4.refs_6_.refs_0_, bf16[704,256]{1,0:T(8,128)(2,1)S(1)} %backward.5.refs_6_.refs_1_, ...), custom_call_target="tpu_custom_call", output_to_operand_aliasing={{1}: (22, {})} | custom-call | flops 1 | bytes 1 | tf_op jit(solution)/shard_map/module_rows/pallas_call | solution.py:323
  168.2 2.6 %module_rows.15 = (bf16[704,512]{1,0:T(8,128)(2,1)}, bf16[1,2,704,2048]{3,2,1,0:T(8,128)(2,1)}) custom-call(s32[9]{0:T(128)S(1)} %pad_add_fusion._, bf16[704,256]{1,0:T(8,128)(2,1)S(1)} %backward.4.refs_6_.refs_0_, bf16[704,256]{1,0:T(8,128)(2,1)S(1)} %backward.5.refs_6_.refs_1_, ...), custom_call_target="tpu_custom_call", output_to_operand_aliasing={{1}: (22, {})} | custom-call | flops 1 | bytes 1 | tf_op jit(solution)/shard_map/module_rows/pallas_call | solution.py:323
  174.6 4.7 %module_rows.17 = (bf16[1,2,704,2048]{3,2,1,0:T(8,128)(2,1)}, f32[2,4,704,512]{3,2,1,0:T(8,128)}, f32[2,4,704,512]{3,2,1,0:T(8,128)}) custom-call(s32[9]{0:T(128)S(1)} %pad_add_fusion._, bf16[704,256]{1,0:T(8,128)(2,1)S(1)} %get-tuple-element.104.refs_6_.refs_0_, ...), custom_call_target="tpu_custom_call", output_to_operand_aliasing={{0}: (21, {})} | custom-call | flops 1 | bytes 1 | tf_op jit(solution)/shard_map/module_rows/pallas_call | solution.py:323
  179.3 4.7 %module_rows.18 = (bf16[1,2,704,2048]{3,2,1,0:T(8,128)(2,1)}, f32[2,4,704,512]{3,2,1,0:T(8,128)}, f32[2,4,704,512]{3,2,1,0:T(8,128)}) custom-call(s32[9]{0:T(128)S(1)} %pad_add_fusion._, bf16[704,256]{1,0:T(8,128)(2,1)S(1)} %backward.4.refs_6_.refs_0_, ...), custom_call_target="tpu_custom_call", output_to_operand_aliasing={{0}: (21, {}), {1}: (24, {}), {2}: (25, {})} | custom-call | flops 1 | bytes 1 | tf_op jit(solution)/shard_map/module_rows/pallas_call | solution.py:323
  184.1 3.8 %module_rows.19 = (f32[2,4,704,512]{3,2,1,0:T(8,128)}, f32[2,4,704,512]{3,2,1,0:T(8,128)}) custom-call(s32[9]{0:T(128)S(1)} %pad_add_fusion._, bf16[704,256]{1,0:T(8,128)(2,1)S(1)} %collective-permute-done.39.refs_0_, bf16[256,512]{1,0:T(8,128)(2,1)S(1)} %collective-permute-done.54.refs_1_, ...), custom_call_target="tpu_custom_call", output_to_operand_aliasing={{0}: (6, {}), {1}: (7, {})} | custom-call | flops 1 | bytes 1 | tf_op jit(solution)/shard_map/module_rows/pallas_call | solution.py:323
  187.9 3.6 %outer_rows.4 = (f32[2,4,704,512]{3,2,1,0:T(8,128)}, f32[2,4,704,512]{3,2,1,0:T(8,128)}) custom-call(s32[9]{0:T(128)S(1)} %pad_add_fusion._, bf16[704,512]{1,0:T(8,128)(2,1)S(1)} %collective-permute-done.53.refs_0_, f32[2,4,704,512]{3,2,1,0:T(8,128)} %bitcast.45, f32[2,4,704,512]{3,2,1,0:T(8,128)} %bitcast.55, ...), custom_call_target="tpu_custom_call", output_to_operand_aliasing={{0}: (4, {}), {1}: (5, {})} | custom-call | flops 1 | bytes 1 | tf_op jit(solution)/shard_map/outer_rows/pallas_call | solution.py:388
  191.6 3.4 %collective-permute-done.52.refs_0_ = bf16[704,512]{1,0:T(8,128)(2,1)} collective-permute-done((bf16[704,512]{1,0:T(8,128)(2,1)}, bf16[704,512]{1,0:T(8,128)(2,1)}, u32[]{:S(2)}, u32[]{:S(2)}) %collective-permute-start.52) | collective-permute-done | bytes 720928 | tf_op jit(solution)/shard_map/ppermute | solution.py:422
  195.0 3.8 %outer_rows.5 = (f32[2,4,704,512]{3,2,1,0:T(8,128)}, f32[2,4,704,512]{3,2,1,0:T(8,128)}) custom-call(s32[9]{0:T(128)S(1)} %pad_add_fusion._, bf16[704,512]{1,0:T(8,128)(2,1)} %collective-permute-done.52.refs_0_, f32[2,4,704,512]{3,2,1,0:T(8,128)} %bitcast.46, f32[2,4,704,512]{3,2,1,0:T(8,128)} %bitcast.56, ...), custom_call_target="tpu_custom_call", output_to_operand_aliasing={{0}: (4, {}), {1}: (5, {})} | custom-call | flops 1 | bytes 1 | tf_op jit(solution)/shard_map/outer_rows/pallas_call | solution.py:388
  198.8 6.4 %outer_rows.6 = (f32[2,4,704,512]{3,2,1,0:T(8,128)}, f32[2,4,704,512]{3,2,1,0:T(8,128)}) custom-call(s32[9]{0:T(128)S(1)} %pad_add_fusion._, bf16[704,512]{1,0:T(8,128)(2,1)} %collective-permute-done.50.refs_0_, bf16[704,512]{1,0:T(8,128)(2,1)S(1)} %collective-permute-done.51.refs_1_, ...), custom_call_target="tpu_custom_call", output_to_operand_aliasing={{0}: (5, {}), {1}: (6, {})} | custom-call | flops 1 | bytes 1 | tf_op jit(solution)/shard_map/outer_rows/pallas_call | solution.py:388
  205.7 3.6 %outer_rows.7 = (f32[2,4,704,512]{3,2,1,0:T(8,128)}, f32[2,4,704,512]{3,2,1,0:T(8,128)}) custom-call(s32[9]{0:T(128)S(1)} %pad_add_fusion._, bf16[704,512]{1,0:T(8,128)(2,1)S(1)} %collective-permute-done.49.refs_0_, f32[2,4,704,512]{3,2,1,0:T(8,128)} %bitcast.48, f32[2,4,704,512]{3,2,1,0:T(8,128)} %bitcast.58, ...), custom_call_target="tpu_custom_call", output_to_operand_aliasing={{0}: (4, {}), {1}: (5, {})} | custom-call | flops 1 | bytes 1 | tf_op jit(solution)/shard_map/outer_rows/pallas_call | solution.py:388
  (131 shorter events, 85.7 us)
Async XLA Ops:
  1.7 15.2 %collective-permute-start.3 = (bf16[64,2048]{1,0:T(8,128)(2,1)S(1)}, bf16[64,2048]{1,0:T(8,128)(2,1)S(1)}, u32[]{:S(2)}, u32[]{:S(2)}) collective-permute-start(bf16[64,2048]{1,0:T(8,128)(2,1)S(1)} %get-tuple-element.187.refs_1_.refs_5_), channel_id=1, source_target_pairs={{0,1},{1,0},{2,3},{3,2},{4,5},{5,4},{6,7},{7,6},{8,9},{9,8},{10,11... | collective-permute-start | bytes 786440 | tf_op jit(solution)/shard_map/ppermute | solution.py:419
  4.7 12.2 %collective-permute-start.2 = (bf16[64,2048]{1,0:T(8,128)(2,1)S(1)}, bf16[64,2048]{1,0:T(8,128)(2,1)S(1)}, u32[]{:S(2)}, u32[]{:S(2)}) collective-permute-start(bf16[64,2048]{1,0:T(8,128)(2,1)S(1)} %get-tuple-element.187.refs_1_.refs_5_), channel_id=1, source_target_pairs={{0,2},{1,3},{2,4},{3,5},{4,6},{5,7},{6,0},{7,1},{8,10},{9,11},{10,... | collective-permute-start | bytes 786440 | tf_op jit(solution)/shard_map/ppermute | solution.py:416
  10.8 24.7 %collective-permute-start.10 = (bf16[704,512]{1,0:T(8,128)(2,1)S(1)}, bf16[704,512]{1,0:T(8,128)(2,1)S(1)}, u32[]{:S(2)}, u32[]{:S(2)}) collective-permute-start(bf16[704,512]{1,0:T(8,128)(2,1)S(1)} %get-tuple-element.94), channel_id=1, source_target_pairs={{0,24},{8,16},{16,8},{24,0},{1,25},{9,17},{17,9},{25,1},{2,26},{10... | collective-permute-start | bytes 2162696 | tf_op jit(solution)/shard_map/ppermute | solution.py:422
  11.8 11.0 %collective-permute-start = (bf16[64,2048]{1,0:T(8,128)(2,1)S(1)}, bf16[64,2048]{1,0:T(8,128)(2,1)S(1)}, u32[]{:S(2)}, u32[]{:S(2)}) collective-permute-start(bf16[64,2048]{1,0:T(8,128)(2,1)S(1)} %get-tuple-element.188.refs_0_.refs_4_), channel_id=1, source_target_pairs={{0,2},{1,3},{2,4},{3,5},{4,6},{5,7},{6,0},{7,1},{8,10},{9,11},{10,... | collective-permute-start | bytes 786440 | tf_op jit(solution)/shard_map/ppermute | solution.py:416
  18.5 11.4 %collective-permute-start.8 = (bf16[64,2048]{1,0:T(8,128)(2,1)S(1)}, bf16[64,2048]{1,0:T(8,128)(2,1)S(1)}, u32[]{:S(2)}, u32[]{:S(2)}) collective-permute-start(bf16[64,2048]{1,0:T(8,128)(2,1)S(1)} %collective-permute-done.2.refs_1_.refs_9_), channel_id=1, source_target_pairs={{0,2},{1,3},{2,4},{3,5},{4,6},{5,7},{6,0},{7,1},{8,10},{9,11},{10,... | collective-permute-start | bytes 786440 | tf_op jit(solution)/shard_map/ppermute | solution.py:416
  26.3 29.1 %collective-permute-start.15 = (bf16[704,512]{1,0:T(8,128)(2,1)S(1)}, bf16[704,512]{1,0:T(8,128)(2,1)S(1)}, u32[]{:S(2)}, u32[]{:S(2)}) collective-permute-start(bf16[704,512]{1,0:T(8,128)(2,1)S(1)} %get-tuple-element.95), channel_id=1, source_target_pairs={{0,24},{8,16},{16,8},{24,0},{1,25},{9,17},{17,9},{25,1},{2,26},{10... | collective-permute-start | bytes 2162696 | tf_op jit(solution)/shard_map/ppermute | solution.py:422
  29.9 12.6 %collective-permute-start.12 = (bf16[64,2048]{1,0:T(8,128)(2,1)S(1)}, bf16[64,2048]{1,0:T(8,128)(2,1)S(1)}, u32[]{:S(2)}, u32[]{:S(2)}) collective-permute-start(bf16[64,2048]{1,0:T(8,128)(2,1)S(1)} %collective-permute-done.8.refs_1_.refs_13_), channel_id=1, source_target_pairs={{0,1},{1,0},{2,3},{3,2},{4,5},{5,4},{6,7},{7,6},{8,9},{9,8},{10,11... | collective-permute-start | bytes 786440 | tf_op jit(solution)/shard_map/ppermute | solution.py:419
  31.7 12.3 %collective-permute-start.11 = (bf16[64,2048]{1,0:T(8,128)(2,1)S(1)}, bf16[64,2048]{1,0:T(8,128)(2,1)S(1)}, u32[]{:S(2)}, u32[]{:S(2)}) collective-permute-start(bf16[64,2048]{1,0:T(8,128)(2,1)S(1)} %collective-permute-done.8.refs_1_.refs_13_), channel_id=1, source_target_pairs={{0,2},{1,3},{2,4},{3,5},{4,6},{5,7},{6,0},{7,1},{8,10},{9,11},{10,... | collective-permute-start | bytes 786440 | tf_op jit(solution)/shard_map/ppermute | solution.py:416
  35.5 12.8 %collective-permute-start.6 = (bf16[64,2048]{1,0:T(8,128)(2,1)S(1)}, bf16[64,2048]{1,0:T(8,128)(2,1)S(1)}, u32[]{:S(2)}, u32[]{:S(2)}) collective-permute-start(bf16[64,2048]{1,0:T(8,128)(2,1)S(1)} %collective-permute-done.4.refs_0_.refs_12_), channel_id=1, source_target_pairs={{0,2},{1,3},{2,4},{3,5},{4,6},{5,7},{6,0},{7,1},{8,10},{9,11},{10,... | collective-permute-start | bytes 786440 | tf_op jit(solution)/shard_map/ppermute | solution.py:416
  42.5 11.3 %collective-permute-start.16 = (bf16[64,2048]{1,0:T(8,128)(2,1)S(1)}, bf16[64,2048]{1,0:T(8,128)(2,1)S(1)}, u32[]{:S(2)}, u32[]{:S(2)}) collective-permute-start(bf16[64,2048]{1,0:T(8,128)(2,1)S(1)} %get-tuple-element.119), channel_id=1, source_target_pairs={{0,2},{1,3},{2,4},{3,5},{4,6},{5,7},{6,0},{7,1},{8,10},{9,11},{10,... | collective-permute-start | bytes 786440 | tf_op jit(solution)/shard_map/ppermute | solution.py:416
  43.9 11.2 %collective-permute-start.21 = (bf16[64,2048]{1,0:T(8,128)(2,1)S(1)}, bf16[64,2048]{1,0:T(8,128)(2,1)S(1)}, u32[]{:S(2)}, u32[]{:S(2)}) collective-permute-start(bf16[64,2048]{1,0:T(8,128)(2,1)S(1)} %get-tuple-element.129), channel_id=1, source_target_pairs={{0,1},{1,0},{2,3},{3,2},{4,5},{5,4},{6,7},{7,6},{8,9},{9,8},{10,11... | collective-permute-start | bytes 786440 | tf_op jit(solution)/shard_map/ppermute | solution.py:419
  53.9 19.1 %collective-permute-start.20 = (bf16[704,512]{1,0:T(8,128)(2,1)S(1)}, bf16[704,512]{1,0:T(8,128)(2,1)S(1)}, u32[]{:S(2)}, u32[]{:S(2)}) collective-permute-start(bf16[704,512]{1,0:T(8,128)(2,1)S(1)} %get-tuple-element.96), channel_id=1, source_target_pairs={{0,16},{8,24},{16,0},{24,8},{1,17},{9,25},{17,1},{25,9},{2,18},{10... | collective-permute-start | bytes 2162696 | tf_op jit(solution)/shard_map/ppermute | solution.py:422
  55.2 17.9 %collective-permute-start.19 = (bf16[64,2048]{1,0:T(8,128)(2,1)S(1)}, bf16[64,2048]{1,0:T(8,128)(2,1)S(1)}, u32[]{:S(2)}, u32[]{:S(2)}) collective-permute-start(bf16[64,2048]{1,0:T(8,128)(2,1)S(1)} %get-tuple-element.126), channel_id=1, source_target_pairs={{0,2},{1,3},{2,4},{3,5},{4,6},{5,7},{6,0},{7,1},{8,10},{9,11},{10,... | collective-permute-start | bytes 786440 | tf_op jit(solution)/shard_map/ppermute | solution.py:416
  60.2 13.2 %collective-permute-start.18 = (bf16[64,2048]{1,0:T(8,128)(2,1)S(1)}, bf16[64,2048]{1,0:T(8,128)(2,1)S(1)}, u32[]{:S(2)}, u32[]{:S(2)}) collective-permute-start(bf16[64,2048]{1,0:T(8,128)(2,1)S(1)} %get-tuple-element.124), channel_id=1, source_target_pairs={{0,1},{1,0},{2,3},{3,2},{4,5},{5,4},{6,7},{7,6},{8,9},{9,8},{10,11... | collective-permute-start | bytes 786440 | tf_op jit(solution)/shard_map/ppermute | solution.py:419
  60.9 10.9 %collective-permute-start.28 = (bf16[64,2048]{1,0:T(8,128)(2,1)S(1)}, bf16[64,2048]{1,0:T(8,128)(2,1)S(1)}, u32[]{:S(2)}, u32[]{:S(2)}) collective-permute-start(bf16[64,2048]{1,0:T(8,128)(2,1)S(1)} %add_rows.1.refs_7_), channel_id=1, source_target_pairs={{0,1},{1,0},{2,3},{3,2},{4,5},{5,4},{6,7},{7,6},{8,9},{9,8},{10,11... | collective-permute-start | bytes 786440 | tf_op jit(solution)/shard_map/ppermute | solution.py:419
  62.3 12.8 %collective-permute-start.22 = (bf16[64,2048]{1,0:T(8,128)(2,1)S(1)}, bf16[64,2048]{1,0:T(8,128)(2,1)S(1)}, u32[]{:S(2)}, u32[]{:S(2)}) collective-permute-start(bf16[64,2048]{1,0:T(8,128)(2,1)S(1)} %add_convert_fusion.4), channel_id=1, source_target_pairs={{0,2},{1,3},{2,4},{3,5},{4,6},{5,7},{6,0},{7,1},{8,10},{9,11},{10,... | collective-permute-start | bytes 786440 | tf_op jit(solution)/shard_map/ppermute | solution.py:416
  71.8 20.1 %collective-permute-start.31 = (bf16[704,512]{1,0:T(8,128)(2,1)S(1)}, bf16[704,512]{1,0:T(8,128)(2,1)S(1)}, u32[]{:S(2)}, u32[]{:S(2)}) collective-permute-start(bf16[704,512]{1,0:T(8,128)(2,1)S(1)} %get-tuple-element.97), channel_id=1, source_target_pairs={{0,16},{8,24},{16,0},{24,8},{1,17},{9,25},{17,1},{25,9},{2,18},{10... | collective-permute-start | bytes 2162696 | tf_op jit(solution)/shard_map/ppermute | solution.py:422
  73.0 18.9 %collective-permute-start.30 = (bf16[2,704,512]{2,1,0:T(8,128)(2,1)S(1)}, bf16[2,704,512]{2,1,0:T(8,128)(2,1)S(1)}, u32[]{:S(2)}, u32[]{:S(2)}) collective-permute-start(bf16[2,704,512]{2,1,0:T(8,128)(2,1)S(1)} %base_rows.5), channel_id=1, source_target_pairs={{0,8},{8,0},{16,24},{24,16},{1,9},{9,1},{17,25},{25,17},{2,10},{10... | collective-permute-start | bytes 4325384 | tf_op jit(solution)/shard_map/ppermute | solution.py:422
  73.4 14.4 %collective-permute-start.27 = (bf16[64,2048]{1,0:T(8,128)(2,1)S(1)}, bf16[64,2048]{1,0:T(8,128)(2,1)S(1)}, u32[]{:S(2)}, u32[]{:S(2)}) collective-permute-start(bf16[64,2048]{1,0:T(8,128)(2,1)S(1)} %get-tuple-element.136), channel_id=1, source_target_pairs={{0,1},{1,0},{2,3},{3,2},{4,5},{5,4},{6,7},{7,6},{8,9},{9,8},{10,11... | collective-permute-start | bytes 786440 | tf_op jit(solution)/shard_map/ppermute | solution.py:419
  87.7 11.0 %collective-permute-start.25 = (bf16[64,2048]{1,0:T(8,128)(2,1)S(1)}, bf16[64,2048]{1,0:T(8,128)(2,1)S(1)}, u32[]{:S(2)}, u32[]{:S(2)}) collective-permute-start(bf16[64,2048]{1,0:T(8,128)(2,1)S(1)} %add_convert_fusion.2), channel_id=1, source_target_pairs={{0,2},{1,3},{2,4},{3,5},{4,6},{5,7},{6,0},{7,1},{8,10},{9,11},{10,... | collective-permute-start | bytes 786440 | tf_op jit(solution)/shard_map/ppermute | solution.py:416
  91.9 10.7 %collective-permute-start.32 = (bf16[64,2048]{1,0:T(8,128)(2,1)S(1)}, bf16[64,2048]{1,0:T(8,128)(2,1)S(1)}, u32[]{:S(2)}, u32[]{:S(2)}) collective-permute-start(bf16[64,2048]{1,0:T(8,128)(2,1)S(1)} %add_convert_fusion), channel_id=1, source_target_pairs={{0,2},{1,3},{2,4},{3,5},{4,6},{5,7},{6,0},{7,1},{8,10},{9,11},{10,... | collective-permute-start | bytes 786440 | tf_op jit(solution)/shard_map/ppermute | solution.py:416
  103.6 11.0 %collective-permute-start.33 = (bf16[64,2048]{1,0:T(8,128)(2,1)S(1)}, bf16[64,2048]{1,0:T(8,128)(2,1)S(1)}, u32[]{:S(2)}, u32[]{:S(2)}) collective-permute-start(bf16[64,2048]{1,0:T(8,128)(2,1)S(1)} %get-tuple-element.186.refs_0_.refs_3_.refs_4_), channel_id=1, source_target_pairs={{0,2},{1,3},{2,4},{3,5},{4,6},{5,7},{6,0},{7,1},{8,10},{9,11},{10,... | collective-permute-start | bytes 786440 | tf_op jit(solution)/shard_map/ppermute | solution.py:416
  103.6 14.4 %collective-permute-start.36 = (bf16[64,2048]{1,0:T(8,128)(2,1)S(1)}, bf16[64,2048]{1,0:T(8,128)(2,1)S(1)}, u32[]{:S(2)}, u32[]{:S(2)}) collective-permute-start(bf16[64,2048]{1,0:T(8,128)(2,1)S(1)} %get-tuple-element.185.refs_1_.refs_4_.refs_5_), channel_id=1, source_target_pairs={{0,1},{1,0},{2,3},{3,2},{4,5},{5,4},{6,7},{7,6},{8,9},{9,8},{10,11... | collective-permute-start | bytes 786440 | tf_op jit(solution)/shard_map/ppermute | solution.py:419
  105.2 15.1 %collective-permute-start.35 = (bf16[64,2048]{1,0:T(8,128)(2,1)S(1)}, bf16[64,2048]{1,0:T(8,128)(2,1)S(1)}, u32[]{:S(2)}, u32[]{:S(2)}) collective-permute-start(bf16[64,2048]{1,0:T(8,128)(2,1)S(1)} %get-tuple-element.185.refs_1_.refs_4_.refs_5_), channel_id=1, source_target_pairs={{0,2},{1,3},{2,4},{3,5},{4,6},{5,7},{6,0},{7,1},{8,10},{9,11},{10,... | collective-permute-start | bytes 786440 | tf_op jit(solution)/shard_map/ppermute | solution.py:416
  105.2 18.3 %collective-permute-start.39 = (bf16[704,256]{1,0:T(8,128)(2,1)S(1)}, bf16[704,256]{1,0:T(8,128)(2,1)S(1)}, u32[]{:S(2)}, u32[]{:S(2)}) collective-permute-start(bf16[704,256]{1,0:T(8,128)(2,1)S(1)} %get-tuple-element.125.refs_3_), channel_id=1, source_target_pairs={{0,16},{8,24},{16,0},{24,8},{1,17},{9,25},{17,1},{25,9},{2,18},{10... | collective-permute-start | bytes 1081352 | tf_op jit(solution)/shard_map/ppermute | solution.py:422
  142.8 22.8 %collective-permute-start.48 = (bf16[704,512]{1,0:T(8,128)(2,1)S(1)}, bf16[704,512]{1,0:T(8,128)(2,1)S(1)}, u32[]{:S(2)}, u32[]{:S(2)}) collective-permute-start(bf16[704,512]{1,0:T(8,128)(2,1)S(1)} %module_rows.10), channel_id=1, source_target_pairs={{0,16},{8,24},{16,0},{24,8},{1,17},{9,25},{17,1},{25,9},{2,18},{10... | collective-permute-start | bytes 2162696 | tf_op jit(solution)/shard_map/ppermute | solution.py:422
  153.4 17.4 %collective-permute-start.54 = (bf16[256,512]{1,0:T(8,128)(2,1)S(1)}, bf16[256,512]{1,0:T(8,128)(2,1)S(1)}, u32[]{:S(2)}, u32[]{:S(2)}) collective-permute-start(bf16[256,512]{1,0:T(8,128)(2,1)S(1)} %take_columns.1.refs_7_), channel_id=1, source_target_pairs={{0,16},{8,24},{16,0},{24,8},{1,17},{9,25},{17,1},{25,9},{2,18},{10... | collective-permute-start | bytes 786440 | tf_op jit(solution)/shard_map/ppermute | solution.py:422
  158.5 29.5 %collective-permute-start.53 = (bf16[704,512]{1,0:T(8,128)(2,1)}, bf16[704,512]{1,0:T(8,128)(2,1)S(1)}, u32[]{:S(2)}, u32[]{:S(2)}) collective-permute-start(bf16[704,512]{1,0:T(8,128)(2,1)} %get-tuple-element.172), channel_id=1, source_target_pairs={{0,16},{8,24},{16,0},{24,8},{1,17},{9,25},{17,1},{25,9},{2,18},{10... | collective-permute-start | bytes 2162696 | tf_op jit(solution)/shard_map/ppermute | solution.py:422
  164.8 34.0 %collective-permute-start.50 = (bf16[704,512]{1,0:T(8,128)(2,1)S(1)}, bf16[704,512]{1,0:T(8,128)(2,1)}, u32[]{:S(2)}, u32[]{:S(2)}) collective-permute-start(bf16[704,512]{1,0:T(8,128)(2,1)S(1)} %get-tuple-element.169), channel_id=1, source_target_pairs={{0,8},{8,0},{16,24},{24,16},{1,9},{9,1},{17,25},{25,17},{2,10},{10... | collective-permute-start | bytes 2162696 | tf_op jit(solution)/shard_map/ppermute | solution.py:422
  164.8 30.2 %collective-permute-start.52 = (bf16[704,512]{1,0:T(8,128)(2,1)}, bf16[704,512]{1,0:T(8,128)(2,1)}, u32[]{:S(2)}, u32[]{:S(2)}) collective-permute-start(bf16[704,512]{1,0:T(8,128)(2,1)} %get-tuple-element.171), channel_id=1, source_target_pairs={{0,24},{8,16},{16,8},{24,0},{1,25},{9,17},{17,9},{25,1},{2,26},{10... | collective-permute-start | bytes 2162696 | tf_op jit(solution)/shard_map/ppermute | solution.py:422
  168.2 30.6 %collective-permute-start.51 = (bf16[704,512]{1,0:T(8,128)(2,1)}, bf16[704,512]{1,0:T(8,128)(2,1)S(1)}, u32[]{:S(2)}, u32[]{:S(2)}) collective-permute-start(bf16[704,512]{1,0:T(8,128)(2,1)} %get-tuple-element.170), channel_id=1, source_target_pairs={{0,8},{8,0},{16,24},{24,16},{1,9},{9,1},{17,25},{25,17},{2,10},{10... | collective-permute-start | bytes 2162696 | tf_op jit(solution)/shard_map/ppermute | solution.py:422
  170.8 34.9 %collective-permute-start.49 = (bf16[704,512]{1,0:T(8,128)(2,1)}, bf16[704,512]{1,0:T(8,128)(2,1)S(1)}, u32[]{:S(2)}, u32[]{:S(2)}) collective-permute-start(bf16[704,512]{1,0:T(8,128)(2,1)} %get-tuple-element.168), channel_id=1, source_target_pairs={{0,24},{8,16},{16,8},{24,0},{1,25},{9,17},{17,9},{25,1},{2,26},{10... | collective-permute-start | bytes 2162696 | tf_op jit(solution)/shard_map/ppermute | solution.py:422
  (30 other events, 437.3 us)
